TPU v7x, 256 devices: a whole 4x4x8 slice. The times are simulated.
256 devices in a mesh: sec: 2 (over y_lo), lat: 4 (over y_hi, core), lon: 32 (over x, z).
Axes of the slice: x: 4, y: 4 (y_hi: 2, y_lo: 2; y = y_hi * 2 + y_lo), z: 8, core: 2. Of those that a mesh axis runs over, the one named last changes fastest.
Arguments:
- tokens: bfloat16 [2, 48, 384, 512], P('sec', 'lat', 'lon'), may hold values from -6 to 6
- cotangent: bfloat16 [2, 24, 192, 512], P('sec', 'lat', 'lon'), may hold values from -6 to 6
- fine_gain: float32 [512], replicated, may hold values from 0.25 to 1.75
- fine_attend: bfloat16 [512, 1536], replicated, may hold values from -4 to 4
- fine_output: bfloat16 [512, 512], replicated, may hold values from -0.25 to 0.25
- merge_weight: bfloat16 [2048, 512], replicated, may hold values from -0.125 to 0.125
- coarse_gain: float32 [512], replicated, may hold values from 0.25 to 1.75
- coarse_attend: bfloat16 [512, 1536], replicated, may hold values from -4 to 4
- coarse_output: bfloat16 [512, 512], replicated, may hold values from -0.25 to 0.25
Outputs:
- coarse_field: bfloat16 [2, 24, 192, 512], P('sec', 'lat', 'lon')
- token_gradient: bfloat16 [2, 48, 384, 512], P('sec', 'lat', 'lon')
- fine_gain_gradient: float32 [512], P('lon')
- fine_attend_gradient: float32 [512, 1536], P('lon')
- fine_output_gradient: float32 [512, 512], P('lon')
- merge_gradient: float32 [2048, 512], P('lon')
- coarse_gain_gradient: float32 [512], P('lon')
- coarse_attend_gradient: float32 [512, 1536], P('lon')
- coarse_output_gradient: float32 [512, 512], P('lon')
All inputs are finite; a program needn't handle non-finite values.
Results may differ from a plain program's by a relative error of at most 0.04.
Values may be sent and summed in bfloat16 or wider, within the bound.
A program may use at most 128 MiB of HBM per device.

v0:
```python
import math

import jax
import jax.numpy as jnp
from jax import lax
from jax.sharding import PartitionSpec as P

HEADS = 8
RADIUS = 6


EPSILON = 1e-06
NEGATIVE = -1e30
PRECISE = lax.Precision.HIGHEST


def with_halo(value, sides, width, wrap):
    for axis, dim in sides:
        size, length = (lax.axis_size(axis), value.shape[dim])
        up = [(i, (i + 1) % size) for i in range(size if wrap else size - 1)]
        down = [(j, i) for i, j in up]
        last = lax.slice_in_dim(value, length - width, length, axis=dim)
        leading = lax.slice_in_dim(value, 0, width, axis=dim)
        before = lax.ppermute(last, axis, up)
        after = lax.ppermute(leading, axis, down)
        value = jnp.concatenate([before, value, after], axis=dim)
    return value


def to_blocks(field):
    rows, columns, depth = field.shape
    shaped = field.reshape(rows // RADIUS, RADIUS, columns // RADIUS, RADIUS, depth)
    return shaped.transpose(0, 2, 1, 3, 4).reshape(-1, RADIUS * RADIUS, depth)


def from_blocks(blocks, rows, columns):
    depth = blocks.shape[-1]
    shaped = blocks.reshape(rows // RADIUS, columns // RADIUS, RADIUS, RADIUS, depth)
    return shaped.transpose(0, 2, 1, 3, 4).reshape(rows, columns, depth)


def regions(padded):
    rows = padded.shape[0] // RADIUS
    columns = padded.shape[1] // RADIUS
    depth = padded.shape[2]
    shaped = padded.reshape(rows, RADIUS, columns, RADIUS, depth)
    pieces = [
        shaped[first : first + rows - 2, :, second : second + columns - 2]
        for first in range(3)
        for second in range(3)
    ]
    stacked = jnp.stack(pieces, 0).reshape(3, 3, rows - 2, RADIUS, columns - 2, RADIUS, depth)
    return stacked.transpose(2, 4, 0, 3, 1, 5, 6).reshape(
        (rows - 2) * (columns - 2), 9 * RADIUS * RADIUS, depth
    )


def unregions(grads, rows, columns):
    block_rows = rows // RADIUS - 2
    block_cols = columns // RADIUS - 2
    depth = grads.shape[-1]
    shaped = grads.reshape(block_rows, block_cols, 3, RADIUS, 3, RADIUS, depth).transpose(
        2, 4, 0, 3, 1, 5, 6
    )
    summed = jnp.zeros((block_rows + 2, RADIUS, block_cols + 2, RADIUS, depth), grads.dtype)
    for first in range(3):
        for second in range(3):
            summed = summed.at[first : first + block_rows, :, second : second + block_cols].add(
                shaped[first, second]
            )
    return summed.reshape(rows, columns, depth)


def window_mask(valid, block_cols):
    block_rows = valid.shape[0] // RADIUS - 2
    cells = jnp.arange(RADIUS * RADIUS, dtype=jnp.int32)
    places = jnp.arange(9 * RADIUS * RADIUS, dtype=jnp.int32)
    query_row = cells // RADIUS
    query_col = cells % RADIUS
    key_row = places // (3 * RADIUS)
    key_col = places % (3 * RADIUS)
    near_rows = (key_row[None, :] >= query_row[:, None]) & (
        key_row[None, :] <= query_row[:, None] + 2 * RADIUS
    )
    near_cols = (key_col[None, :] >= query_col[:, None]) & (
        key_col[None, :] <= query_col[:, None] + 2 * RADIUS
    )
    shaped = valid.reshape(block_rows + 2, RADIUS)
    bands = jnp.stack([shaped[first : first + block_rows] for first in range(3)], 1).reshape(
        block_rows, 3 * RADIUS
    )
    open_keys = jnp.broadcast_to(bands[:, :, None], (block_rows, 3 * RADIUS, 3 * RADIUS)).reshape(
        block_rows, 9 * RADIUS * RADIUS
    )
    open_keys = jnp.repeat(open_keys, block_cols, axis=0)
    return (near_rows & near_cols)[None, None] & open_keys[:, None, None, :]


def attend(query, keys, values, valid):
    rows, columns, width = query.shape
    head_dim = width // HEADS
    factor = 1.0 / math.sqrt(head_dim)
    count = rows // RADIUS * (columns // RADIUS)
    query_blocks = to_blocks(query).reshape(count, RADIUS * RADIUS, HEADS, head_dim)
    key_blocks = regions(keys).reshape(count, 9 * RADIUS * RADIUS, HEADS, head_dim)
    value_blocks = regions(values).reshape(count, 9 * RADIUS * RADIUS, HEADS, head_dim)
    scores = (
        jnp.einsum("bqnc,bknc->bnqk", query_blocks, key_blocks, preferred_element_type=jnp.float32)
        * factor
    )
    scores = jnp.where(window_mask(valid, columns // RADIUS), scores, NEGATIVE)
    peak = jnp.max(scores, axis=-1, keepdims=True)
    expo = jnp.exp(scores - peak)
    attention = expo / jnp.sum(expo, axis=-1, keepdims=True)
    mixed = jnp.einsum(
        "bnqk,bknc->bqnc",
        attention.astype(jnp.bfloat16),
        value_blocks,
        preferred_element_type=jnp.float32,
    )
    return (from_blocks(mixed.reshape(count, RADIUS * RADIUS, width), rows, columns), attention)


def attend_back(query, keys, values, attention, slope):
    rows, columns, width = query.shape
    head_dim = width // HEADS
    factor = 1.0 / math.sqrt(head_dim)
    count = rows // RADIUS * (columns // RADIUS)
    query_blocks = to_blocks(query).reshape(count, RADIUS * RADIUS, HEADS, head_dim)
    key_blocks = regions(keys).reshape(count, 9 * RADIUS * RADIUS, HEADS, head_dim)
    value_blocks = regions(values).reshape(count, 9 * RADIUS * RADIUS, HEADS, head_dim)
    slope_blocks = to_blocks(slope).reshape(count, RADIUS * RADIUS, HEADS, head_dim)
    prob_slope = jnp.einsum(
        "bqnc,bknc->bnqk", slope_blocks, value_blocks, preferred_element_type=jnp.float32
    )
    score_slope = (
        attention * (prob_slope - jnp.sum(attention * prob_slope, axis=-1, keepdims=True)) * factor
    ).astype(jnp.bfloat16)
    query_slope = jnp.einsum(
        "bnqk,bknc->bqnc", score_slope, key_blocks, preferred_element_type=jnp.float32
    )
    key_slope = jnp.einsum(
        "bnqk,bqnc->bknc", score_slope, query_blocks, preferred_element_type=jnp.float32
    )
    value_slope = jnp.einsum(
        "bnqk,bqnc->bknc",
        attention.astype(jnp.bfloat16),
        slope_blocks,
        preferred_element_type=jnp.float32,
    )
    pair = jnp.concatenate(
        [key_slope.reshape(count, -1, width), value_slope.reshape(count, -1, width)], axis=-1
    )
    wide = unregions(pair, rows + 2 * RADIUS, columns + 2 * RADIUS)
    return (from_blocks(query_slope.reshape(count, RADIUS * RADIUS, width), rows, columns), wide)


def widen(field):
    broad = with_halo(field, (("lon", 1),), RADIUS, True)
    return with_halo(broad, (("lat", 0),), RADIUS, False)


def fold_rows(grad, income):
    inner = grad[RADIUS:-RADIUS]
    inner = inner.at[:RADIUS].add(income[:RADIUS])
    return inner.at[-RADIUS:].add(income[-RADIUS:])


def fold_columns(grad, income):
    inner = grad[:, RADIUS:-RADIUS]
    inner = inner.at[:, :RADIUS].add(income[:, :RADIUS])
    return inner.at[:, -RADIUS:].add(income[:, -RADIUS:])


def narrow(grad):
    edges = jnp.concatenate([grad[:RADIUS], grad[-RADIUS:]], axis=0)
    income = with_halo(edges.astype(jnp.bfloat16), (("lat", 0),), RADIUS, False).astype(edges.dtype)
    grad = fold_rows(grad, income)
    edges = jnp.concatenate([grad[:, :RADIUS], grad[:, -RADIUS:]], axis=1)
    income = with_halo(edges.astype(jnp.bfloat16), (("lon", 1),), RADIUS, True).astype(edges.dtype)
    return fold_columns(grad, income)


def pole_rows(rows):
    start = lax.axis_index("lat") * rows - RADIUS
    places = start + jnp.arange(rows + 2 * RADIUS, dtype=jnp.int32)
    return (places >= 0) & (places < rows * lax.axis_size("lat"))


def normalize(field, gain):
    upcast = field.astype(jnp.float32)
    factor = lax.rsqrt(jnp.mean(upcast * upcast, axis=-1, keepdims=True) + EPSILON)
    normed = upcast * factor
    return (upcast, factor, normed, (normed * gain).astype(jnp.bfloat16))


def layer_forward(field, gain, attend_weight, output_weight):
    rows, columns, width = field.shape
    upcast, factor, normed, hidden = normalize(field, gain)
    flat = hidden.reshape(-1, width)
    projected = jnp.dot(flat, attend_weight, preferred_element_type=jnp.float32)
    projected = projected.astype(jnp.bfloat16).reshape(rows, columns, 3 * width)
    query = projected[..., :width]
    wide = widen(projected[..., width:])
    valid = pole_rows(rows)
    keys = wide[..., :width]
    values = wide[..., width:]
    attended, attention = attend(query, keys, values, valid)
    attended = attended.astype(jnp.bfloat16)
    moved = jnp.dot(attended.reshape(-1, width), output_weight, preferred_element_type=jnp.float32)
    output = (upcast + moved.reshape(rows, columns, width)).astype(jnp.bfloat16)
    return (
        output,
        (factor, normed, hidden, hidden, query, keys, values, valid, attention, attended),
    )


def layer_backward(slope, gain, attend_weight, output_weight, saved):
    factor, normed, hidden, hidden_wide, query, keys, values, valid, attention, attended = saved
    rows, columns, width = slope.shape
    flat_slope = slope.reshape(-1, width)
    output_slope = jnp.dot(
        attended.reshape(-1, width).T, flat_slope, preferred_element_type=jnp.float32
    )
    mixed_slope = jnp.dot(flat_slope, output_weight.T, preferred_element_type=jnp.float32)
    mixed_slope = mixed_slope.astype(jnp.bfloat16).reshape(rows, columns, width)
    query_slope, wide_slope = attend_back(query, keys, values, attention, mixed_slope)
    query_slope = query_slope.reshape(-1, width)
    weights = attend_weight.astype(jnp.float32)
    own_hidden = hidden.reshape(-1, width).astype(jnp.float32)
    pair_slope = narrow(wide_slope).reshape(-1, 2 * width)
    joined = jnp.concatenate([query_slope, pair_slope], axis=1)
    attend_slope = jnp.dot(own_hidden.T, joined, precision=PRECISE)
    hidden_slope = jnp.dot(joined, weights.T, precision=PRECISE)
    hidden_slope = hidden_slope.reshape(rows, columns, width)
    gain_slope = jnp.sum(hidden_slope * normed, axis=(0, 1))
    scaled = hidden_slope * gain
    input_slope = slope.astype(jnp.float32) + factor * (
        scaled - normed * jnp.mean(scaled * normed, axis=-1, keepdims=True)
    )
    return (input_slope, gain_slope, attend_slope, output_slope)


def per_device(
    tokens,
    cotangent,
    fine_gain,
    fine_attend,
    fine_output,
    merge_weight,
    coarse_gain,
    coarse_attend,
    coarse_output,
):
    fine_tile = tokens[0]
    rows, columns, width = fine_tile.shape
    fine_field, fine_saved = layer_forward(fine_tile, fine_gain, fine_attend, fine_output)
    merged = (
        fine_field.reshape(rows // 2, 2, columns // 2, 2, width)
        .transpose(0, 2, 1, 3, 4)
        .reshape(-1, 4 * width)
    )
    coarse_in = jnp.dot(merged, merge_weight, preferred_element_type=jnp.float32)
    coarse_in = coarse_in.astype(jnp.bfloat16).reshape(rows // 2, columns // 2, width)
    coarse_field, coarse_saved = layer_forward(coarse_in, coarse_gain, coarse_attend, coarse_output)
    coarse_slope, coarse_gain_slope, coarse_attend_slope, coarse_output_slope = layer_backward(
        cotangent[0], coarse_gain, coarse_attend, coarse_output, coarse_saved
    )
    coarse_flat = coarse_slope.astype(jnp.bfloat16).reshape(-1, width)
    merge_slope = jnp.dot(merged.T, coarse_flat, preferred_element_type=jnp.float32)
    merged_slope = jnp.dot(coarse_flat, merge_weight.T, preferred_element_type=jnp.float32).astype(
        jnp.bfloat16
    )
    fine_slope = (
        merged_slope.reshape(rows // 2, columns // 2, 2, 2, width)
        .transpose(0, 2, 1, 3, 4)
        .reshape(rows, columns, width)
    )
    token_slope, fine_gain_slope, fine_attend_slope, fine_output_slope = layer_backward(
        fine_slope, fine_gain, fine_attend, fine_output, fine_saved
    )
    shares = (
        lax.psum_scatter(
            fine_gain_slope.astype(jnp.bfloat16), "lon", scatter_dimension=0, tiled=True
        ).astype(jnp.float32),
        lax.psum_scatter(
            fine_attend_slope.astype(jnp.bfloat16), "lon", scatter_dimension=0, tiled=True
        ).astype(jnp.float32),
        lax.psum_scatter(
            fine_output_slope.astype(jnp.bfloat16), "lon", scatter_dimension=0, tiled=True
        ).astype(jnp.float32),
        lax.psum_scatter(
            merge_slope.astype(jnp.bfloat16), "lon", scatter_dimension=0, tiled=True
        ).astype(jnp.float32),
        lax.psum_scatter(
            coarse_gain_slope.astype(jnp.bfloat16), "lon", scatter_dimension=0, tiled=True
        ).astype(jnp.float32),
        lax.psum_scatter(
            coarse_attend_slope.astype(jnp.bfloat16), "lon", scatter_dimension=0, tiled=True
        ).astype(jnp.float32),
        lax.psum_scatter(
            coarse_output_slope.astype(jnp.bfloat16), "lon", scatter_dimension=0, tiled=True
        ).astype(jnp.float32),
    )
    sums = (
        lax.psum(shares[0].astype(jnp.bfloat16), ("sec", "lat")).astype(jnp.float32),
        lax.psum(shares[1].astype(jnp.bfloat16), ("sec", "lat")).astype(jnp.float32),
        lax.psum(shares[2].astype(jnp.bfloat16), ("sec", "lat")).astype(jnp.float32),
        lax.psum(shares[3].astype(jnp.bfloat16), ("sec", "lat")).astype(jnp.float32),
        lax.psum(shares[4].astype(jnp.bfloat16), ("sec", "lat")).astype(jnp.float32),
        lax.psum(shares[5].astype(jnp.bfloat16), ("sec", "lat")).astype(jnp.float32),
        lax.psum(shares[6].astype(jnp.bfloat16), ("sec", "lat")).astype(jnp.float32),
    )
    return (
        coarse_field[None],
        token_slope.astype(jnp.bfloat16)[None],
        sums[0],
        sums[1],
        sums[2],
        sums[3],
        sums[4],
        sums[5],
        sums[6],
    )


def solution(mesh):
    return jax.shard_map(
        per_device,
        mesh=mesh,
        in_specs=(
            P("sec", "lat", "lon", None),
            P("sec", "lat", "lon", None),
            P(),
            P(),
            P(),
            P(),
            P(),
            P(),
            P(),
        ),
        out_specs=(
            P("sec", "lat", "lon", None),
            P("sec", "lat", "lon", None),
            P("lon"),
            P("lon", None),
            P("lon", None),
            P("lon", None),
            P("lon"),
            P("lon", None),
            P("lon", None),
        ),
        check_vma=False,
    )
```

profile of v0, /device:TPU:1, one launch (start us, length us, event | category | flops | bytes accessed | tf_op | source)
XLA Modules:
  0.0 1419.2 jit_solution(13411737086746478346)
XLA Ops:
  15.3 6.1 collective-permute-start.1
  29.1 5.9 collective-permute-start.2
  41.1 3.8 collective-permute-done.3
  58.1 5.3 reshape_reshape.32
  63.5 5.3 copy.217
  71.1 3.0 reshape_reshape.34
  74.1 5.4 copy.216
  79.5 3.6 fusion.139
  89.6 4.9 collective-permute-start.5
  96.2 5.1 collective-permute-done.4
  104.0 5.1 collective-permute-start.6
  126.4 3.4 convolution_bitcast_fusion.4
  146.7 4.4 scatter-add.75
  151.1 3.8 broadcast_select_fusion
  155.0 4.5 scatter-add.76
  161.4 3.2 scatter-add.79
  166.6 3.2 scatter-add.80
  171.7 3.2 scatter-add.81
  176.8 3.2 scatter-add.84
  181.9 3.3 scatter-add.85
  187.2 3.2 scatter-add.86
  200.1 5.6 collective-permute-start.8
  211.1 4.8 collective-permute-start.11
  218.2 3.5 multiply_reduce_fusion.4
  229.2 12.2 convolution_bitcast_fusion.1
  241.4 5.9 copy.273
  247.3 4.4 concatenate.127
  251.7 7.2 copy.271
  259.0 5.6 concatenate.126
  264.6 7.2 maximum_bitcast_fusion
  273.5 2.9 add_select_fusion.1
  276.4 8.3 scatter-add.90
  284.8 3.4 add_select_fusion
  288.2 9.0 scatter-add.91
  302.6 8.1 scatter-add.95
  318.4 7.7 scatter-add.100
  328.8 7.1 collective-permute-start.12
  341.6 4.2 collective-permute-done.13
  348.4 5.1 collective-permute-start.15
  353.5 10.6 fusion.14
  379.7 4.0 multiply_reduce_fusion.2
  383.8 57.7 %all-reduce.4 = (bf16[512]{0:T(512)(128)(2,1)S(1)}, bf16[512]{0:T(512)(128)(2,1)S(1)}) all-reduce(bf16[512]{0:T(512)(128)(2,1)S(1)} %get-tuple-element.353, bf16[512]{0:T(512)(128)(2,1)S(1)} %copy-done.47), channel_id=2, replica_groups=mesh['sec'=2,'lat'=4,'lon'=32] {'lon'}, use_global_device_ids=true, to_apply=%region_13.14.clone | all-reduce | flops 1024 | bytes 4096
  442.7 179.2 %reduce-scatter.8.cloned.1.call-done = bf16[16,512]{1,0:T(8,128)(2,1)} async-done(((bf16[512,512]{1,0:T(8,128)(2,1)}), bf16[16,512]{1,0:T(8,128)(2,1)}) %reduce-scatter.8.cloned.1.call-update) | async-done | bytes 16400 | tf_op jit(solution)/shard_map/reduce_scatter | solution.py:289
  621.9 218.4 %reduce-scatter.12.cloned.1.call-done = bf16[16,1536]{1,0:T(8,128)(2,1)} async-done(((bf16[512,1536]{1,0:T(8,128)(2,1)}), bf16[16,1536]{1,0:T(8,128)(2,1)}) %reduce-scatter.12.cloned.1.call-update) | async-done | bytes 49168 | tf_op jit(solution)/shard_map/reduce_scatter | solution.py:298
  840.4 218.1 %reduce-scatter.6.cloned.1.call-done = bf16[16,1536]{1,0:T(8,128)(2,1)} async-done(((bf16[512,1536]{1,0:T(8,128)(2,1)}), bf16[16,1536]{1,0:T(8,128)(2,1)}) %reduce-scatter.6.cloned.1.call-update) | async-done | bytes 49168 | tf_op jit(solution)/shard_map/reduce_scatter | solution.py:286
  1059.6 217.6 %reduce-scatter.10.cloned.1.call-done = bf16[64,512]{1,0:T(8,128)(2,1)} async-done(((bf16[2048,512]{1,0:T(8,128)(2,1)}), bf16[64,512]{1,0:T(8,128)(2,1)}) %reduce-scatter.10.cloned.1.call-update) | async-done | bytes 65552 | tf_op jit(solution)/shard_map/reduce_scatter | solution.py:292
  1279.1 66.6 %all-reduce.11.cloned.1.call-done = (bf16[16]{0:T(256)(128)(2,1)}, bf16[16,1536]{1,0:T(8,128)(2,1)}, bf16[16,512]{1,0:T(8,128)(2,1)}, bf16[16]{0:T(256)(128)(2,1...) async-done(((bf16[16]{0:T(256)(128)(2,1)}, bf16[16,1536]{1,0:T(8,128)(2,1)}, bf16[16,512]{1,0:T(8,128)(2,1)}, bf16[16]{0:T(256)(128)(2,1)}, ...) | async-done | bytes 131152 | tf_op jit(solution)/shard_map/psum | solution.py:306
  1353.4 57.3 %all-reduce.9.cloned.1.call-done = bf16[64,512]{1,0:T(8,128)(2,1)} async-done(((bf16[64,512]{1,0:T(8,128)(2,1)}), bf16[64,512]{1,0:T(8,128)(2,1)}) %all-reduce.9.cloned.1.call-update) | async-done | bytes 65552 | tf_op jit(solution)/shard_map/psum | solution.py:309
  (369 shorter events, 171.8 us)
Async XLA Ops:
  7.2 80.5 %copy-start = (bf16[2048,512]{1,0:T(8,128)(2,1)S(1)}, bf16[2048,512]{1,0:T(8,128)(2,1)}, u32[]{:S(2)}) copy-start(bf16[2048,512]{1,0:T(8,128)(2,1)} %param.74) | copy-start | bytes 6291460
  7.2 435.5 %reduce-scatter.14.cloned.1.call-start = ((), (), s32[]{:S(2)}) async-start(), calls=%async_computation.10 | async-start | bytes 540672 | tf_op jit(solution)/shard_map/reduce_scatter | solution.py:301
  9.4 3.5 copy-start.5
  11.9 11.3 copy-start.35
  12.8 13.4 collective-permute-start
  15.3 11.6 collective-permute-start.1
  22.2 15.8 %copy-start.20 = (bf16[12,12,512]{2,1,0:T(8,128)(2,1)S(1)}, bf16[12,12,512]{2,1,0:T(8,128)(2,1)}, u32[]{:S(2)}) copy-start(bf16[12,12,512]{2,1,0:T(8,128)(2,1)} %slice.1355) | copy-start | bytes 442372
  29.1 12.0 collective-permute-start.2
  35.1 9.9 collective-permute-start.3
  39.2 5.7 copy-start.42
  50.0 4.8 copy-start.2
  74.1 5.4 copy-start.28
  74.1 5.4 copy-start.34
  88.2 23.0 %copy-start.48 = (s32[5]{0:T(128)S(1)}, s32[5]{0:T(128)}, u32[]{:S(2)}) copy-start(s32[5]{0:T(128)} %concatenate.121) | copy-start | bytes 64
  88.2 22.9 %copy-start.49 = (s32[5]{0:T(128)S(1)}, s32[5]{0:T(128)}, u32[]{:S(2)}) copy-start(s32[5]{0:T(128)} %constant.771.clone.1) | copy-start | bytes 64
  89.6 6.5 collective-permute-start.5
  94.5 6.8 collective-permute-start.4
  102.1 11.2 collective-permute-start.7
  104.0 9.3 collective-permute-start.6
  119.4 2.9 copy-start.33
  119.4 2.9 copy-start.41
  119.8 4.6 copy-start.13
  126.4 3.4 copy-start.51
  190.4 4.6 copy-start.32
  190.4 5.4 copy-start.31
  196.6 9.2 copy-start.30
  198.2 10.2 collective-permute-start.9
  200.1 9.3 collective-permute-start.8
  206.9 415.0 %reduce-scatter.8.cloned.1.call-start = ((), (), s32[]{:S(2)}) async-start(), calls=%async_computation.6 | async-start | bytes 540672 | tf_op jit(solution)/shard_map/reduce_scatter | solution.py:289
  208.1 7.7 copy-start.27
  211.0 7.2 copy-start.37
  211.0 7.2 copy-start.46
  211.0 6.9 collective-permute-start.10
  211.1 6.8 collective-permute-start.11
  284.8 12.4 copy-start.17
  301.0 539.4 %reduce-scatter.12.cloned.1.call-start = ((), (), s32[]{:S(2)}) async-start(), calls=%async_computation.9 | async-start | bytes 1622016 | tf_op jit(solution)/shard_map/reduce_scatter | solution.py:298
  316.8 741.6 %reduce-scatter.6.cloned.1.call-start = ((), (), s32[]{:S(2)}) async-start(), calls=%async_computation.5 | async-start | bytes 1622016 | tf_op jit(solution)/shard_map/reduce_scatter | solution.py:286
  328.8 12.8 collective-permute-start.12
  336.2 9.7 collective-permute-start.13
  348.3 16.5 %collective-permute-start.14 = (bf16[12,6,1024]{2,1,0:T(8,128)(2,1)S(1)}, bf16[12,6,1024]{2,1,0:T(8,128)(2,1)}, u32[]{:S(2)}, u32[]{:S(2)}) collective-permute-start(bf16[12,6,1024]{2,1,0:T(8,128)(2,1)S(1)} %get-tuple-element.379), channel_id=1, source_target_pairs={{0,1},{1,2},{2,3},{3,4},{4,5},{5,6},{6,7},{7,8},{8,9},{9,10},{10,1... | collective-permute-start | bytes 442376 | tf_op jit(solution)/shard_map/ppermute | solution.py:24
  348.4 16.4 %collective-permute-start.15 = (bf16[12,6,1024]{2,1,0:T(8,128)(2,1)S(1)}, bf16[12,6,1024]{2,1,0:T(8,128)(2,1)}, u32[]{:S(2)}, u32[]{:S(2)}) collective-permute-start(bf16[12,6,1024]{2,1,0:T(8,128)(2,1)S(1)} %get-tuple-element.380), channel_id=1, source_target_pairs={{1,0},{2,1},{3,2},{4,3},{5,4},{6,5},{7,6},{8,7},{9,8},{10,9},{11,1... | collective-permute-start | bytes 442376 | tf_op jit(solution)/shard_map/ppermute | solution.py:25
  374.3 3.5 copy-start.23
  374.3 902.9 %reduce-scatter.10.cloned.1.call-start = ((), (), s32[]{:S(2)}) async-start(), calls=%async_computation.7 | async-start | bytes 2162688 | tf_op jit(solution)/shard_map/reduce_scatter | solution.py:292
  376.5 969.1 %all-reduce.11.cloned.1.call-start = ((), (), s32[]{:S(2)}) async-start(), calls=%async_computation.11 | async-start | bytes 264192 | tf_op jit(solution)/shard_map/psum | solution.py:306
  378.8 5.0 copy-start.47
  379.7 897.5 %copy-start.9 = (bf16[1,12,12,512]{3,2,1,0:T(8,128)(2,1)S(1)}, bf16[1,12,12,512]{3,2,1,0:T(8,128)(2,1)}, u32[]{:S(2)}) copy-start(bf16[1,12,12,512]{3,2,1,0:T(8,128)(2,1)} %param.69) | copy-start | bytes 442372
  379.7 1032.5 %copy-start.1 = (bf16[2048,512]{1,0:T(8,128)(2,1)S(1)}, bf16[2048,512]{1,0:T(8,128)(2,1)}, u32[]{:S(2)}) copy-start(bf16[2048,512]{1,0:T(8,128)(2,1)} %param.74) | copy-start | bytes 6291460
  1058.4 352.3 %all-reduce.9.cloned.1.call-start = ((), (), s32[]{:S(2)}) async-start(), calls=%async_computation.8 | async-start | bytes 131072 | tf_op jit(solution)/shard_map/psum | solution.py:309
  (30 other events, 43.7 us)
Sparse Core Ops, SparseCore 0:
  207.1 199.7 reduce-scatter.13
  411.1 210.7 reduce-scatter.7
  625.7 214.5 reduce-scatter.11
  844.0 214.3 reduce-scatter.5
  1062.1 215.0 reduce-scatter.9
  1280.6 64.9 all-reduce.10
  1347.9 62.7 all-reduce.8
where the time goes:
time: 1430 us; the launch traced here: 1420 us
  waiting for transfers between devices  976 us (68%)
  local copies, waits for them, and re-layouts  172 us (12%)
  other arithmetic  72.2 us (5%)
  matrix products  69.7 us (5%)
  blocking collectives  57.7 us (4%)
  starting transfers between devices  55.3 us (4%)
  between operations  16.6 us (1%)
    reduce_scatter x1, waiting for transfers between devices, per_device(): lax.psum_scatter(coarse_attend_slope.astype(jnp.bfloat16), 'lon', scatter...  218 us
    reduce_scatter x1, waiting for transfers between devices, per_device(): lax.psum_scatter(fine_attend_slope.astype(jnp.bfloat16), 'lon', scatter_d...  218 us
    reduce_scatter x1, waiting for transfers between devices, per_device(): lax.psum_scatter(merge_slope.astype(jnp.bfloat16), 'lon', scatter_dimensi...  218 us
    reduce_scatter x1, waiting for transfers between devices, per_device(): lax.psum_scatter(fine_output_slope.astype(jnp.bfloat16), 'lon', scatter_d...  179 us
    psum x1, waiting for transfers between devices, per_device(): lax.psum(shares[0].astype(jnp.bfloat16), ('sec', 'lat')).astype(jnp.float32)  66.6 us
    scatter-add x14, local copies, waits for them, and re-layouts, unregions(): summed.at[first:first + block_rows, :, second:second + block_cols]  63.4 us
    unnamed x1, blocking collectives  57.7 us
    psum x1, waiting for transfers between devices, per_device(): lax.psum(shares[3].astype(jnp.bfloat16), ('sec', 'lat')).astype(jnp.float32)  57.3 us
  transfers between devices with their start and end apart: 23, of which 14 were waited for; matrix products, arithmetic and copies ran while one was open for 12% of the time, Pallas kernels for 0%

commit v1 on v0

v1 whole, which is shorter than its diff:
```python
import functools

import jax
import jax.numpy as jnp
import numpy as np
from jax import lax
from jax.experimental import pallas as pl
from jax.experimental.pallas import tpu as pltpu
from jax.sharding import PartitionSpec as P

HEADS = 8
RADIUS = 6
EPSILON = 1e-06
NEGATIVE = -1e30
UNIT = 48
D = 512
PAIRS = 4
MESH = pl.DeviceIdType.MESH
F32 = jnp.float32
BF16 = jnp.bfloat16
AROUND = ((0, 1), (0, -1), (1, 0), (-1, 0), (1, 1), (1, -1), (-1, 1), (-1, -1))


def dot(left, right):
    return jnp.dot(left, right, preferred_element_type=F32)


def dot_t(left, right):
    return lax.dot_general(left, right, (((1,), (1,)), ((), ())), preferred_element_type=F32)


def t_dot(left, right):
    return lax.dot_general(left, right, (((0,), (0,)), ((), ())), preferred_element_type=F32)


def window_bias():
    query = np.arange(UNIT)
    row, col = query // 8, query % 8
    key = np.arange(9 * UNIT)
    unit, cell = key // UNIT, key % UNIT
    key_row = unit // 3 * RADIUS + cell // 8
    key_col = unit % 3 * RADIUS + cell % 8
    near = (
        (key_row[None] >= row[:, None])
        & (key_row[None] <= row[:, None] + 2 * RADIUS)
        & (key_col[None] >= col[:, None])
        & (key_col[None] <= col[:, None] + 2 * RADIUS)
        & (cell % 8 < RADIUS)[None]
    )
    bias = np.where(near, 0.0, NEGATIVE).astype(np.float32)
    return np.concatenate([bias, bias], 0)


def merge_matrix():
    matrix = np.zeros((4 * UNIT, 4 * UNIT), np.float32)
    for a in range(2):
        for b in range(2):
            for i in range(RADIUS):
                for j in range(RADIUS):
                    r, c = 2 * i + a, 2 * j + b
                    place = (r // 6 * 2 + c // 6) * UNIT + r % 6 * 8 + c % 6
                    matrix[(a * 2 + b) * UNIT + i * 8 + j, place] = 1.0
    return matrix


class Layout:
    def __init__(self, mesh):
        self.sec, self.lat, self.lon = (mesh.shape[k] for k in ("sec", "lat", "lon"))
        self.x = 4 if self.lon == 32 else 2
        self.z = self.lon // self.x
        self.y_hi = self.lat // 2
        self.y = self.y_hi * self.sec
        self.blocks = self.lon
        self.depth = D // self.blocks
        self.z_low = self.z // 2
        self.fine_width = 2048 // (2 * self.y)
        self.coarse_width = 4096 // (2 * self.y)


def unit_window(width, starts, ref, column):
    return jnp.concatenate([ref[pl.ds(s, width), pl.ds(column, 128)] for s in starts], 0)


def low_lanes(rows):
    return lax.broadcasted_iota(jnp.int32, (rows, 128), 1) < 64


def stack_heads(part):
    part = part.astype(F32)
    low = low_lanes(UNIT)
    return jnp.concatenate([jnp.where(low, part, 0.0), jnp.where(low, 0.0, part)], 0).astype(BF16)


def merge_heads(both):
    return jnp.where(low_lanes(UNIT), both[:UNIT], both[UNIT:])


def attend(query, keys, values, bias):
    scores = dot_t(query, keys) * 0.125 + bias
    expo = jnp.exp(scores - jnp.max(scores, axis=-1, keepdims=True))
    attention = expo / jnp.sum(expo, axis=-1, keepdims=True)
    return attention, merge_heads(dot(attention.astype(BF16), values))


def attend_back(query, keys, values, attention, slope):
    prob = dot_t(slope, values)
    mean = jnp.sum(attention * prob, axis=-1, keepdims=True)
    score = (attention * (prob - mean) * 0.125).astype(BF16)
    query_slope = merge_heads(dot(score, keys))
    key_slope = t_dot(score, query)
    value_slope = t_dot(attention.astype(BF16), slope)
    return query_slope, key_slope, value_slope


def norm(field, gain):
    factor = lax.rsqrt(jnp.mean(field * field, axis=-1, keepdims=True) + EPSILON)
    normed = field * factor
    return factor, normed, (normed * gain).astype(BF16)


def input_back(slope, hidden_slope, field, gain):
    factor = lax.rsqrt(jnp.mean(field * field, axis=-1, keepdims=True) + EPSILON)
    normed = field * factor
    scaled = hidden_slope * gain
    return slope + factor * (scaled - normed * jnp.mean(scaled * normed, axis=-1, keepdims=True))


class Reducer:
    def __init__(self, lay, place, wires, refs):
        self.lay, self.place, self.wires = lay, place, wires
        (
            self.given, self.pair_in, self.pair_sum,
            self.in_1a, self.in_1b, self.sum_2a, self.sum_2b,
            self.in_2a, self.in_2b, self.sum_3, self.in_3, self.full,
        ) = refs
        self.copies = []

    def device(self, core=None, y=None, x=None, z=None):
        here = self.place
        core = here["core"] if core is None else core
        y = here["y"] if y is None else y
        x = here["x"] if x is None else x
        z = here["z"] if z is None else z
        return (y % self.lay.sec, y // self.lay.sec * 2 + core, x * self.lay.z + z)

    def send(self, source, target, device):
        copy = self.wires(source, target, device)
        copy.start()
        self.copies.append(copy)

    def arrive(self):
        for copy in self.copies:
            copy.wait()
        self.copies = []

    def pair_start(self):
        other = 1 - self.place["core"]
        self.send(self.given.at[other], self.pair_in, self.device(core=other))

    def pair_finish(self):
        self.arrive()
        core = self.place["core"]
        span = self.lay.x

        @pl.loop(0, self.lay.y * span)
        def _(step):
            y, x = step // span, step % span
            total = self.given[core, y, x].astype(F32) + self.pair_in[y, x].astype(F32)
            self.pair_sum[y, x] = total.astype(BF16)

    def first_start(self):
        lay, here = self.lay, self.place
        low = pl.ds(0, lay.z_low)
        high = pl.ds(lay.z_low, lay.z - lay.z_low)
        for step in range(1, lay.x):
            x = (here["x"] + step) % lay.x
            self.send(self.pair_sum.at[:, x, low], self.in_1a.at[step - 1], self.device(x=x))
        for step in range(1, lay.y):
            y = (here["y"] + step) % lay.y
            self.send(self.pair_sum.at[y, :, high], self.in_1b.at[step - 1], self.device(y=y))

    def first_finish(self):
        self.arrive()
        lay, here = self.lay, self.place
        low = pl.ds(0, lay.z_low)
        high = pl.ds(lay.z_low, lay.z - lay.z_low)

        @pl.loop(0, lay.y)
        def _(y):
            total = self.pair_sum[y, here["x"], low].astype(F32)
            for k in range(lay.x - 1):
                total += self.in_1a[k, y].astype(F32)
            self.sum_2a[y] = total.astype(BF16)

        @pl.loop(0, lay.x)
        def _(x):
            total = self.pair_sum[here["y"], x, high].astype(F32)
            for k in range(lay.y - 1):
                total += self.in_1b[k, x].astype(F32)
            self.sum_2b[x] = total.astype(BF16)

    def second_start(self):
        lay, here = self.lay, self.place
        for step in range(1, lay.y):
            y = (here["y"] + step) % lay.y
            self.send(self.sum_2a.at[y], self.in_2a.at[step - 1], self.device(y=y))
        for step in range(1, lay.x):
            x = (here["x"] + step) % lay.x
            self.send(self.sum_2b.at[x], self.in_2b.at[step - 1], self.device(x=x))

    def second_finish(self):
        self.arrive()
        lay, here = self.lay, self.place
        total = self.sum_2a[here["y"]].astype(F32)
        for k in range(lay.y - 1):
            total += self.in_2a[k].astype(F32)
        self.sum_3[pl.ds(0, lay.z_low)] = total.astype(BF16)
        total = self.sum_2b[here["x"]].astype(F32)
        for k in range(lay.x - 1):
            total += self.in_2b[k].astype(F32)
        self.sum_3[pl.ds(lay.z_low, lay.z - lay.z_low)] = total.astype(BF16)

    def third_start(self):
        lay, here = self.lay, self.place
        for step in range(1, lay.z):
            z = (here["z"] + step) % lay.z
            self.send(self.sum_3.at[z], self.in_3.at[step - 1], self.device(z=z))

    def third_finish(self):
        self.arrive()
        lay, here = self.lay, self.place
        total = self.sum_3[here["z"]].astype(F32)
        for k in range(lay.z - 1):
            total += self.in_3[k].astype(F32)
        self.full[here["core"], here["y"]] = total.astype(BF16)

    def last_start(self):
        lay, here = self.lay, self.place
        own = self.full.at[here["core"], here["y"]]
        for across in range(2):
            for step in range(lay.y):
                if across or step:
                    core = (here["core"] + across) % 2
                    y = (here["y"] + step) % lay.y
                    self.send(own, own, self.device(core=core, y=y))

    def last_finish(self):
        self.arrive()

    def column(self, start, width):
        size = self.full.shape[-1]
        parts = []
        while width > 0:
            group, offset = divmod(start, size)
            take = min(width, size - offset)
            parts.append(self.full[group // self.lay.y, group % self.lay.y, :, offset : offset + take])
            start, width = start + take, width - take
        return (parts[0] if len(parts) == 1 else jnp.concatenate(parts, 1)).astype(F32)

    def put(self, start, product):
        lay = self.lay
        size = self.given.shape[-1]
        done, width = 0, product.shape[1]
        while done < width:
            group, offset = divmod(start + done, size)
            take = min(width - done, size - offset)
            piece = product[:, done : done + take].astype(BF16)
            self.given[group // lay.y, group % lay.y, :, :, :, offset : offset + take] = piece.reshape(
                lay.x, lay.z, lay.depth, take
            )
            done += take

    def put_merged(self, part, start, product):
        lay = self.lay
        size = self.given.shape[-1]
        count = lay.blocks // 4
        shaped = product.astype(BF16).reshape(count, 4, lay.depth, D)
        for run in range(4):
            group, offset = divmod(start + run * D, size)
            for block in range(count):
                x, z = divmod(part * count + block, lay.z)
                self.given[group // lay.y, group % lay.y, x, z, :, offset : offset + D] = shaped[block, run]


def kernel(
    lay,
    tokens, cotangent, fine_gain, coarse_gain, bias_ref, merge_ref, split_ref,
    fine_attend_hbm, fine_output_hbm, merge_hbm, coarse_attend_hbm, coarse_output_hbm,
    coarse_field, token_gradient,
    fine_gain_out, fine_attend_out, fine_output_out, merge_out,
    coarse_gain_out, coarse_attend_out, coarse_output_out,
    fine_attend, fine_output, merge_weight, coarse_attend, coarse_output,
    strip, field_f, wide_f, pairs_f, query_f, hidden_f, attention_f, mixed_f, merged,
    slope_f, mixed_slope_f, wide_slope_f, rims_f, query_slope_f,
    from_lon, from_lat, from_corner,
    field_c, wide_c, pairs_c, query_c, hidden_c, attention_c, mixed_c,
    slope_c, rims_c, query_slope_c, pair_slope_c, from_around,
    *rest,
):
    coarse_refs, fine_refs = rest[:12], rest[12:24]
    load_sem, send_sem, recv_sem = rest[24:]
    sec, lat, lon = (lax.axis_index(k) for k in ("sec", "lat", "lon"))
    place = {
        "core": lat % 2,
        "y": lat // 2 * lay.sec + sec,
        "x": lon // lay.z,
        "z": lon % lay.z,
    }
    used = [0]

    def wires(source, target, device):
        index = used[0]
        used[0] += 1
        return pltpu.make_async_remote_copy(
            src_ref=source,
            dst_ref=target,
            send_sem=send_sem.at[index],
            recv_sem=recv_sem.at[index],
            device_id=device,
            device_id_type=MESH,
        )

    def neighbour(step):
        return (sec, (lat + step[0] + lay.lat) % lay.lat, (lon + step[1] + lay.lon) % lay.lon)

    coarse_sum = Reducer(lay, place, wires, coarse_refs)
    fine_sum = Reducer(lay, place, wires, fine_refs)

    loads = [
        pltpu.make_async_copy(source, target, load_sem.at[i])
        for i, (source, target) in enumerate(
            (
                (fine_attend_hbm, fine_attend),
                (fine_output_hbm, fine_output),
                (merge_hbm, merge_weight),
                (coarse_attend_hbm, coarse_attend),
                (coarse_output_hbm, coarse_output),
            )
        )
    ]
    for load in loads:
        load.start()

    barrier = pltpu.get_barrier_semaphore()
    peers = [neighbour(step) for step in AROUND]
    peers += [coarse_sum.device(x=(place["x"] + s) % lay.x) for s in range(1, lay.x)]
    peers += [coarse_sum.device(z=(place["z"] + s) % lay.z) for s in range(1, lay.z)]
    peers += [
        coarse_sum.device(core=(place["core"] + c) % 2, y=(place["y"] + s) % lay.y)
        for c in range(2)
        for s in range(lay.y)
        if c or s
    ]
    for peer in peers:
        pl.semaphore_signal(barrier, inc=1, device_id=peer, device_id_type=MESH)

    field_f[...] = jnp.zeros_like(field_f)
    field_c[...] = jnp.zeros_like(field_c)
    for row in range(12):
        strip[row, :12] = tokens[0, row].astype(F32)
    for row in range(12):
        for half in range(2):
            place_of = (row // 6 * 2 + half) * UNIT + row % 6 * 8
            field_f[place_of : place_of + 6] = strip[row, 6 * half : 6 * half + 6]
    for unit in range(4):
        wide_f[1 + unit // 2, 1 + unit % 2] = field_f[unit * UNIT : (unit + 1) * UNIT].astype(BF16)
    for row in range(6):
        field_c[row * 8 : row * 8 + 6] = cotangent[0, row].astype(F32)
    slope_c[...] = field_c[...]

    pl.semaphore_wait(barrier, len(peers))

    def wide_part(step, mine):
        index = []
        for way in step:
            if way == 0:
                index.append(pl.ds(1, 2))
            elif way > 0:
                index.append(2 if mine else 3)
            else:
                index.append(1 if mine else 0)
        return tuple(index)

    def opposite(step):
        return (-step[0], -step[1])

    halo = []
    for step in AROUND:
        copy = wires(
            wide_f.at[wide_part(step, True)],
            wide_f.at[wide_part(opposite(step), False)],
            neighbour(step),
        )
        copy.start()
        halo.append(copy)

    top = jnp.where(lat == 0, NEGATIVE, 0.0)
    bottom = jnp.where(lat == lay.lat - 1, NEGATIVE, 0.0)
    lanes = lax.broadcasted_iota(jnp.int32, (1, 9 * UNIT), 1)

    def bias_at(is_first, is_last):
        above = jnp.where(is_first, top, 0.0)
        below = jnp.where(is_last, bottom, 0.0)
        rim = jnp.where(lanes < 3 * UNIT, above, 0.0) + jnp.where(lanes >= 6 * UNIT, below, 0.0)
        return bias_ref[...] + rim

    gain_f = fine_gain[...]
    gain_c = coarse_gain[...]
    loads[0].wait()
    hidden_f[...] = norm(field_f[...], gain_f)[2]
    query_f[...] = dot(hidden_f[...], fine_attend[:, :D]).astype(BF16)
    for copy in halo:
        copy.wait()

    @pl.loop(0, 4)
    def _(row):
        field = wide_f[row].reshape(4 * UNIT, D).astype(F32)
        hidden = norm(field, gain_f)[2]
        pairs_f[pl.ds(pl.multiple_of(row * 4 * UNIT, 4 * UNIT), 4 * UNIT), :] = dot(
            hidden, fine_attend[:, D:]
        ).astype(BF16)

    def starts_of(quad):
        first, second = quad // 2, quad % 2
        return [pl.multiple_of(((first + i) * 4 + second) * UNIT, UNIT) for i in range(3)]

    @pl.loop(0, 4)
    def _(quad):
        first = quad // 2
        own = pl.ds(pl.multiple_of(quad * UNIT, UNIT), UNIT)
        bias = bias_at(first == 0, first == 1)
        starts = starts_of(quad)
        for pair in range(PAIRS):
            query = stack_heads(query_f[own, pair * 128 : pair * 128 + 128])
            keys = unit_window(3 * UNIT, starts, pairs_f, pair * 128)
            values = unit_window(3 * UNIT, starts, pairs_f, D + pair * 128)
            attention, mixed = attend(query, keys, values, bias)
            attention_f[quad, pair] = attention
            mixed_f[own, pair * 128 : pair * 128 + 128] = mixed.astype(BF16)

    loads[1].wait()
    fine_field = (field_f[...] + dot(mixed_f[...], fine_output[...])).astype(BF16)
    merged[...] = dot(merge_ref[...], fine_field).astype(BF16)
    loads[2].wait()
    coarse_in = jnp.zeros((UNIT, D), F32)
    for part in range(4):
        coarse_in += dot(merged[part * UNIT : (part + 1) * UNIT], merge_weight[part * D : (part + 1) * D])
    wide_c[1, 1] = coarse_in.astype(BF16)

    halo = []
    for step in AROUND:
        copy = wires(wide_c.at[1, 1], wide_c.at[1 - step[0], 1 - step[1]], neighbour(step))
        copy.start()
        halo.append(copy)

    loads[3].wait()
    loads[4].wait()
    field_c[...] = wide_c[1, 1].astype(F32)
    hidden_c[...] = norm(field_c[...], gain_c)[2]
    query_c[...] = dot(hidden_c[...], coarse_attend[:, :D]).astype(BF16)
    mixed_slope_c = dot_t(slope_c[...].astype(BF16), coarse_output[...]).astype(BF16)
    for copy in halo:
        copy.wait()
    hidden = norm(wide_c[...].reshape(9 * UNIT, D).astype(F32), gain_c)[2]
    pairs_c[...] = dot(hidden, coarse_attend[:, D:]).astype(BF16)
    bias = bias_at(True, True)
    for pair in range(PAIRS):
        low, high = pair * 128, pair * 128 + 128
        query = stack_heads(query_c[:, low:high])
        keys, values = pairs_c[:, low:high], pairs_c[:, D + low : D + high]
        attention, mixed = attend(query, keys, values, bias)
        mixed_c[:, low:high] = mixed.astype(BF16)
        query_slope, key_slope, value_slope = attend_back(
            query, keys, values, attention, stack_heads(mixed_slope_c[:, low:high])
        )
        query_slope_c[:, low:high] = query_slope.astype(BF16)
        pair_slope_c[:, low:high] = key_slope[4 * UNIT : 5 * UNIT]
        pair_slope_c[:, D + low : D + high] = value_slope[4 * UNIT : 5 * UNIT]
        rims_c[:, :, low:high] = key_slope.astype(BF16).reshape(9, UNIT, 128)
        rims_c[:, :, D + low : D + high] = value_slope.astype(BF16).reshape(9, UNIT, 128)

    halo = []
    for index, step in enumerate(AROUND):
        source = rims_c.at[(1 + step[0]) * 3 + 1 + step[1]]
        copy = wires(source, from_around.at[index], neighbour(step))
        copy.start()
        halo.append(copy)

    moved = field_c[...] + dot(mixed_c[...], coarse_output[...])
    for row in range(6):
        coarse_field[0, row] = moved[row * 8 : row * 8 + 6].astype(BF16)
    slope_flat = slope_c[...].astype(BF16)
    coarse_sum.put(1536, t_dot(mixed_c[...], slope_flat))
    coarse_sum.put(0, t_dot(hidden_c[...], query_slope_c[...]))
    for copy in halo:
        copy.wait()
    pair_slope = pair_slope_c[...]
    for index in range(8):
        pair_slope += from_around[index].astype(F32)
    pair_slope = pair_slope.astype(BF16)
    coarse_sum.put(512, t_dot(hidden_c[...], pair_slope[:, :D]))
    coarse_sum.put(1024, t_dot(hidden_c[...], pair_slope[:, D:]))
    hidden_slope = dot_t(query_slope_c[...], coarse_attend[:, :D]) + dot_t(pair_slope, coarse_attend[:, D:])
    coarse_slope = input_back(slope_c[...], hidden_slope, field_c[...], gain_c).astype(BF16)
    for part in range(4):
        piece = merged[part * UNIT : (part + 1) * UNIT]
        coarse_sum.put_merged(part, 2048, t_dot(piece, coarse_slope))
    merged_slope = jnp.concatenate(
        [dot_t(coarse_slope, merge_weight[part * D : (part + 1) * D]).astype(BF16) for part in range(4)], 0
    )
    coarse_sum.pair_start()

    slope_f[...] = dot(split_ref[...], merged_slope).astype(BF16)
    mixed_slope_f[...] = dot_t(slope_f[...], fine_output[...]).astype(BF16)
    fine_sum.put(1536, t_dot(mixed_f[...], slope_f[...]))
    wide_slope_f[...] = jnp.zeros_like(wide_slope_f)
    coarse_sum.pair_finish()
    coarse_sum.first_start()

    @pl.loop(0, 4)
    def _(quad):
        own = pl.ds(pl.multiple_of(quad * UNIT, UNIT), UNIT)
        starts = starts_of(quad)
        for pair in range(PAIRS):
            low, high = pair * 128, pair * 128 + 128
            query = stack_heads(query_f[own, low:high])
            slope = stack_heads(mixed_slope_f[own, low:high])
            keys = unit_window(3 * UNIT, starts, pairs_f, low)
            values = unit_window(3 * UNIT, starts, pairs_f, D + low)
            query_slope, key_slope, value_slope = attend_back(
                query, keys, values, attention_f[quad, pair], slope
            )
            query_slope_f[own, low:high] = query_slope.astype(BF16)
            for i, start in enumerate(starts):
                rows = pl.ds(start, 3 * UNIT)
                part = slice(i * 3 * UNIT, (i + 1) * 3 * UNIT)
                wide_slope_f[rows, low:high] += key_slope[part]
                wide_slope_f[rows, D + low : D + high] += value_slope[part]

    @pl.loop(0, 16)
    def _(unit):
        rows = pl.ds(pl.multiple_of(unit * UNIT, UNIT), UNIT)
        rims_f[unit // 4, unit % 4] = wide_slope_f[rows, :].astype(BF16)

    targets = {}
    for index, step in enumerate(AROUND):
        if step[0] == 0:
            targets[step] = from_lon.at[index]
        elif step[1] == 0:
            targets[step] = from_lat.at[index - 2]
        else:
            targets[step] = from_corner.at[index - 4]
    halo = []
    for step in AROUND:
        copy = wires(rims_f.at[wide_part(step, False)], targets[step], neighbour(step))
        copy.start()
        halo.append(copy)
    coarse_sum.first_finish()
    coarse_sum.second_start()
    fine_sum.put(0, t_dot(hidden_f[...], query_slope_f[...]))
    for copy in halo:
        copy.wait()
    coarse_sum.second_finish()
    coarse_sum.third_start()

    for index, step in enumerate(AROUND):
        for k in range(4):
            first, second = divmod(k, 2)
            if step[0] and first != (0 if step[0] > 0 else 1):
                continue
            if step[1] and second != (0 if step[1] > 0 else 1):
                continue
            row = ((1 + first) * 4 + 1 + second) * UNIT
            if step[0] == 0:
                piece = from_lon[index, first]
            elif step[1] == 0:
                piece = from_lat[index - 2, second]
            else:
                piece = from_corner[index - 4]
            wide_slope_f[row : row + UNIT, :] += piece.astype(F32)
    centre = [wide_slope_f[r * UNIT : (r + 2) * UNIT, :].astype(BF16) for r in (5, 9)]
    pair_slope = jnp.concatenate(centre, 0)
    fine_sum.put(512, t_dot(hidden_f[...], pair_slope[:, :D]))
    fine_sum.put(1024, t_dot(hidden_f[...], pair_slope[:, D:]))
    fine_sum.pair_start()
    hidden_slope = dot_t(query_slope_f[...], fine_attend[:, :D]) + dot_t(pair_slope, fine_attend[:, D:])
    slope = input_back(slope_f[...].astype(F32), hidden_slope, field_f[...], gain_f)
    for row in range(12):
        for half in range(2):
            place_of = (row // 6 * 2 + half) * UNIT + row % 6 * 8
            strip[row, 6 * half : 6 * half + 6] = slope[place_of : place_of + 6]
    for row in range(12):
        token_gradient[0, row] = strip[row, :12].astype(BF16)

    fine_sum.pair_finish()
    fine_sum.first_start()
    coarse_sum.third_finish()
    coarse_sum.last_start()
    fine_sum.first_finish()
    fine_sum.second_start()
    coarse_sum.last_finish()

    def gain_back(total, weight, gain):
        own = weight[pl.ds(pl.multiple_of(lon * lay.depth, lay.depth), lay.depth), :].astype(F32)
        column = jnp.sum(total * own, axis=1, keepdims=True)
        row = lax.broadcasted_iota(jnp.int32, (lay.depth, D), 0) + lon * lay.depth
        at = lax.broadcasted_iota(jnp.int32, (lay.depth, D), 1) == row
        column = column / jnp.sum(jnp.where(at, gain, 0.0), axis=1, keepdims=True)
        square = (lay.depth, lay.depth)
        same = lax.broadcasted_iota(jnp.int32, square, 0) == lax.broadcasted_iota(jnp.int32, square, 1)
        return jnp.sum(jnp.where(same, column, 0.0), axis=0, keepdims=True)

    total = coarse_sum.column(0, 1536)
    coarse_attend_out[...] = total
    coarse_gain_out[...] = gain_back(total, coarse_attend, gain_c)
    coarse_output_out[...] = coarse_sum.column(1536, D)
    for run in range(4):
        merge_out[run * lay.depth : (run + 1) * lay.depth, :] = coarse_sum.column(2048 + run * D, D)

    fine_sum.second_finish()
    fine_sum.third_start()
    fine_sum.third_finish()
    fine_sum.last_start()
    fine_sum.last_finish()
    total = fine_sum.column(0, 1536)
    fine_attend_out[...] = total
    fine_gain_out[...] = gain_back(total, fine_attend, gain_f)
    fine_output_out[...] = fine_sum.column(1536, D)


def reducer_scratch(lay, width):
    y, x, z, low = lay.y, lay.x, lay.z, lay.z_low
    high = z - low
    end = (lay.depth, width)
    shapes = (
        (2, y, x, z), (y, x, z), (y, x, z),
        (x - 1, y, low), (y - 1, x, high), (y, low), (x, high),
        (y - 1, low), (x - 1, high), (z,), (z - 1,), (2, y),
    )
    return [pltpu.VMEM(shape + end, BF16) for shape in shapes]


def per_device(
    lay,
    tokens,
    cotangent,
    fine_gain,
    fine_attend,
    fine_output,
    merge_weight,
    coarse_gain,
    coarse_attend,
    coarse_output,
):
    vmem = pl.BlockSpec(memory_space=pltpu.VMEM)
    hbm = pl.BlockSpec(memory_space=pl.ANY)
    select = merge_matrix()
    per_batch = 1 + 2 * (lay.x - 1 + lay.y - 1) + lay.z - 1 + 2 * lay.y - 1
    copies = 4 * 8 + 2 * per_batch
    depth = lay.depth
    outs = pl.pallas_call(
        functools.partial(kernel, lay),
        out_shape=(
            jax.ShapeDtypeStruct(cotangent.shape, BF16),
            jax.ShapeDtypeStruct(tokens.shape, BF16),
            jax.ShapeDtypeStruct((1, depth), F32),
            jax.ShapeDtypeStruct((depth, 3 * D), F32),
            jax.ShapeDtypeStruct((depth, D), F32),
            jax.ShapeDtypeStruct((4 * depth, D), F32),
            jax.ShapeDtypeStruct((1, depth), F32),
            jax.ShapeDtypeStruct((depth, 3 * D), F32),
            jax.ShapeDtypeStruct((depth, D), F32),
        ),
        in_specs=[vmem] * 7 + [hbm] * 5,
        out_specs=[vmem] * 9,
        scratch_shapes=[
            pltpu.VMEM((D, 3 * D), BF16),
            pltpu.VMEM((D, D), BF16),
            pltpu.VMEM((4 * D, D), BF16),
            pltpu.VMEM((D, 3 * D), BF16),
            pltpu.VMEM((D, D), BF16),
            pltpu.VMEM((12, 16, D), F32),
            pltpu.VMEM((4 * UNIT, D), F32),
            pltpu.VMEM((4, 4, UNIT, D), BF16),
            pltpu.VMEM((16 * UNIT, 2 * D), BF16),
            pltpu.VMEM((4 * UNIT, D), BF16),
            pltpu.VMEM((4 * UNIT, D), BF16),
            pltpu.VMEM((4, PAIRS, 2 * UNIT, 9 * UNIT), F32),
            pltpu.VMEM((4 * UNIT, D), BF16),
            pltpu.VMEM((4 * UNIT, D), BF16),
            pltpu.VMEM((4 * UNIT, D), BF16),
            pltpu.VMEM((4 * UNIT, D), BF16),
            pltpu.VMEM((16 * UNIT, 2 * D), F32),
            pltpu.VMEM((4, 4, UNIT, 2 * D), BF16),
            pltpu.VMEM((4 * UNIT, D), BF16),
            pltpu.VMEM((2, 2, UNIT, 2 * D), BF16),
            pltpu.VMEM((2, 2, UNIT, 2 * D), BF16),
            pltpu.VMEM((4, UNIT, 2 * D), BF16),
            pltpu.VMEM((UNIT, D), F32),
            pltpu.VMEM((3, 3, UNIT, D), BF16),
            pltpu.VMEM((9 * UNIT, 2 * D), BF16),
            pltpu.VMEM((UNIT, D), BF16),
            pltpu.VMEM((UNIT, D), BF16),
            pltpu.VMEM((2 * UNIT, 9 * UNIT), F32),
            pltpu.VMEM((UNIT, D), BF16),
            pltpu.VMEM((UNIT, D), F32),
            pltpu.VMEM((9, UNIT, 2 * D), BF16),
            pltpu.VMEM((UNIT, D), BF16),
            pltpu.VMEM((UNIT, 2 * D), F32),
            pltpu.VMEM((8, UNIT, 2 * D), BF16),
            *reducer_scratch(lay, lay.coarse_width),
            *reducer_scratch(lay, lay.fine_width),
            pltpu.SemaphoreType.DMA((5,)),
            pltpu.SemaphoreType.DMA((copies,)),
            pltpu.SemaphoreType.DMA((copies,)),
        ],
        compiler_params=pltpu.CompilerParams(
            collective_id=0, has_side_effects=True, vmem_limit_bytes=56 * 1024 * 1024
        ),
    )(
        tokens,
        cotangent,
        fine_gain.reshape(1, D),
        coarse_gain.reshape(1, D),
        jnp.asarray(window_bias()),
        jnp.asarray(select, BF16),
        jnp.asarray(select.T, BF16),
        fine_attend,
        fine_output,
        merge_weight,
        coarse_attend,
        coarse_output,
    )
    outs = list(outs)
    outs[2] = outs[2].reshape(depth)
    outs[6] = outs[6].reshape(depth)
    return tuple(outs)


def solution(mesh):
    return jax.shard_map(
        functools.partial(per_device, Layout(mesh)),
        mesh=mesh,
        in_specs=(
            P("sec", "lat", "lon", None),
            P("sec", "lat", "lon", None),
            P(),
            P(),
            P(),
            P(),
            P(),
            P(),
            P(),
        ),
        out_specs=(
            P("sec", "lat", "lon", None),
            P("sec", "lat", "lon", None),
            P("lon"),
            P("lon", None),
            P("lon", None),
            P("lon", None),
            P("lon"),
            P("lon", None),
            P("lon", None),
        ),
        check_vma=False,
    )
```

time: 1430 us -> 127 us (0.09)
  waiting for transfers between devices: 976 us -> 0 us
  local copies, waits for them, and re-layouts: 172 us -> 12.7 us
  Pallas kernels: 0 us -> 113 us
  other arithmetic: 72.2 us -> 0 us
  matrix products: 69.7 us -> 0 us
  blocking collectives: 57.7 us -> 0 us
  starting transfers between devices: 55.3 us -> 0 us
  between operations: 16.6 us -> 0.66 us
    reduce_scatter x5 -> x0, waiting for transfers between devices: 833 us -> none  [the longest x1 218 us: per_device(): lax.psum_scatter(coarse_attend_slope.astype(jnp.bfloat16), 'lon', scatter...]
    psum x2 -> x0, waiting for transfers between devices: 124 us -> none  [the longest x1 66.6 us: per_device(): lax.psum(shares[0].astype(jnp.bfloat16), ('sec', 'lat')).astype(jnp.float32)]
    pallas_call x0 -> x1, Pallas kernels: none -> 113 us  [per_device(): pl.pallas_call(functools.partial(kernel, lay), out_shape=(jax.ShapeDtypeS...]
    scatter-add x16 -> x0, local copies, waits for them, and re-layouts: 66.9 us -> none  [the longest x14 63.4 us: unregions(): summed.at[first:first + block_rows, :, second:second + block_cols]]
    dot_general x25 -> x0, matrix products: 64 us -> none  [the longest x2 14.7 us: attend_back(): jnp.einsum('bnqk,bqnc->bknc', score_slope, query_blocks, preferred_elemen...]
    unnamed x1 -> x0, blocking collectives: 57.7 us -> none
    ppermute x16 -> x0, starting transfers between devices: 55 us -> none  [the longest x8 28.5 us: with_halo(): after = lax.ppermute(leading, axis, down)]
    another operation x33 -> x0, local copies, waits for them, and re-layouts: 34.8 us -> none
  transfers between devices with their start and end apart: 23 -> 0, of which waited for: 14 -> 0; matrix products, arithmetic and copies ran while one was open for 12% -> 0% of each run, Pallas kernels for 0% -> 0%
where the time goes in v1:
time: 127 us; the launch traced here: 126 us
  Pallas kernels  113 us (89%)
  local copies, waits for them, and re-layouts  12.7 us (10%)
    pallas_call x1, Pallas kernels, per_device(): pl.pallas_call(functools.partial(kernel, lay), out_shape=(jax.ShapeDtypeS...  113 us
    unnamed x9, local copies, waits for them, and re-layouts  12.7 us

profile of v1, /device:TPU:1, one launch (start us, length us, event | category | flops | bytes accessed | tf_op | source)
XLA Modules:
  0.0 126.1 jit_solution(11035743653927824095)
XLA Ops:
  0.6 112.8 %shard_map.187 = (bf16[1,6,6,512]{3,2,1,0:T(8,128)(2,1)}, bf16[1,12,12,512]{3,2,1,0:T(8,128)(2,1)}, f32[1,16]{1,0:T(1,128)}, f32[16,1536]{1,0:T(8,128)}, f32[16,...) custom-call(bf16[1,12,12,512]{3,2,1,0:T(8,128)(2,1)} %tokens.1, ...), custom_call_target="tpu_custom_call" | custom-call | tf_op jit(solution)/shard_map/pallas_call | solution.py:661
  113.4 1.4 %copy.30 = bf16[1,6,6,512]{3,2,1,0:T(8,128)(2,1)} copy(bf16[1,6,6,512]{3,2,1,0:T(8,128)(2,1)} %get-tuple-element.36) | data formatting | bytes 73728
  114.8 1.6 %copy.31 = bf16[1,12,12,512]{3,2,1,0:T(8,128)(2,1)} copy(bf16[1,12,12,512]{3,2,1,0:T(8,128)(2,1)} %get-tuple-element.37) | data formatting | bytes 294912
  116.4 1.1 copy.32
  117.6 1.5 %copy.33 = f32[16,1536]{1,0:T(8,128)} copy(f32[16,1536]{1,0:T(8,128)} %get-tuple-element.39) | data formatting | bytes 196608
  119.1 1.4 %copy.34 = f32[16,512]{1,0:T(8,128)} copy(f32[16,512]{1,0:T(8,128)} %get-tuple-element.40) | data formatting | bytes 65536
  120.5 1.6 %copy.35 = f32[64,512]{1,0:T(8,128)} copy(f32[64,512]{1,0:T(8,128)} %get-tuple-element.41) | data formatting | bytes 262144
  122.1 1.2 copy.36
  123.2 1.5 %copy.37 = f32[16,1536]{1,0:T(8,128)} copy(f32[16,1536]{1,0:T(8,128)} %get-tuple-element.43) | data formatting | bytes 196608
  124.8 1.4 %copy.38 = f32[16,512]{1,0:T(8,128)} copy(f32[16,512]{1,0:T(8,128)} %get-tuple-element.44) | data formatting | bytes 65536

commit v2 on v1

v2 whole, which is shorter than its diff:
```python
import functools

import jax
import jax.numpy as jnp
import numpy as np
from jax import lax
from jax.experimental import pallas as pl
from jax.experimental.pallas import tpu as pltpu
from jax.sharding import PartitionSpec as P

HEADS = 8
RADIUS = 6
EPSILON = 1e-06
NEGATIVE = -1e30
UNIT = 48
D = 512
PAIRS = 4
MESH = pl.DeviceIdType.MESH
F32 = jnp.float32
BF16 = jnp.bfloat16
AROUND = ((0, 1), (0, -1), (1, 0), (-1, 0), (1, 1), (1, -1), (-1, 1), (-1, -1))


def dot(left, right):
    return jnp.dot(left, right, preferred_element_type=F32)


def dot_t(left, right):
    return lax.dot_general(left, right, (((1,), (1,)), ((), ())), preferred_element_type=F32)


def t_dot(left, right):
    return lax.dot_general(left, right, (((0,), (0,)), ((), ())), preferred_element_type=F32)


def near_window():
    query = np.arange(UNIT)
    row, col = query // 8, query % 8
    key = np.arange(9 * UNIT)
    unit, cell = key // UNIT, key % UNIT
    key_row = unit // 3 * RADIUS + cell // 8
    key_col = unit % 3 * RADIUS + cell % 8
    return (
        (key_row[None] >= row[:, None])
        & (key_row[None] <= row[:, None] + 2 * RADIUS)
        & (key_col[None] >= col[:, None])
        & (key_col[None] <= col[:, None] + 2 * RADIUS)
        & (cell % 8 < RADIUS)[None]
    )


def window_bias():
    bias = np.where(near_window(), 0.0, NEGATIVE).astype(np.float32)
    return np.concatenate([bias, bias], 0)


def window_bias_back():
    used = (np.arange(UNIT) % 8 < RADIUS)[:, None]
    bias = np.where(near_window() & used, 0.0, NEGATIVE).astype(np.float32).T
    return np.concatenate([bias, bias], 1)


def head_columns():
    matrix = np.zeros((D, 128), np.float32)
    for head in range(HEADS):
        matrix[head * 64 : head * 64 + 64, head * 8 : head * 8 + 6] = 1.0
    return matrix


def statistic_columns():
    matrix = np.zeros((2, PAIRS, 2 * UNIT, 128), np.float32)
    for which in range(2):
        for head in range(HEADS):
            pair, side = divmod(head, 2)
            start = head * 8 + 3 * which
            matrix[which, pair, side * UNIT : (side + 1) * UNIT, start : start + 3] = 1.0
    return matrix


def merge_matrix():
    matrix = np.zeros((4 * UNIT, 4 * UNIT), np.float32)
    for a in range(2):
        for b in range(2):
            for i in range(RADIUS):
                for j in range(RADIUS):
                    r, c = 2 * i + a, 2 * j + b
                    place = (r // 6 * 2 + c // 6) * UNIT + r % 6 * 8 + c % 6
                    matrix[(a * 2 + b) * UNIT + i * 8 + j, place] = 1.0
    return matrix


class Layout:
    def __init__(self, mesh):
        self.sec, self.lat, self.lon = (mesh.shape[k] for k in ("sec", "lat", "lon"))
        self.x = 4 if self.lon == 32 else 2
        self.z = self.lon // self.x
        self.y_hi = self.lat // 2
        self.y = self.y_hi * self.sec
        self.blocks = self.lon
        self.depth = D // self.blocks
        self.z_low = self.z // 2
        self.fine_width = 1024 // (2 * self.y)
        self.coarse_width = 4096 // (2 * self.y)


def unit_window(width, starts, ref, column):
    return jnp.concatenate([ref[pl.ds(s, width), pl.ds(column, 128)] for s in starts], 0)


def low_lanes(rows):
    return lax.broadcasted_iota(jnp.int32, (rows, 128), 1) < 64


def stack_heads(part):
    part = part.astype(F32)
    low = low_lanes(UNIT)
    return jnp.concatenate([jnp.where(low, part, 0.0), jnp.where(low, 0.0, part)], 0).astype(BF16)


def merge_heads(both):
    return jnp.where(low_lanes(UNIT), both[:UNIT], both[UNIT:])


def attend(query, keys, values, bias):
    scores = dot_t(query, keys) * 0.125 + bias
    peak = jnp.max(scores, axis=-1, keepdims=True)
    expo = jnp.exp(scores - peak)
    total = jnp.sum(expo, axis=-1, keepdims=True)
    attention = expo / total
    return attention, merge_heads(dot(attention.astype(BF16), values)), peak + jnp.log(total)


def query_back(keys, values, attention, slope):
    prob = dot_t(slope, values)
    mean = jnp.sum(attention * prob, axis=-1, keepdims=True)
    score = (attention * (prob - mean) * 0.125).astype(BF16)
    return merge_heads(dot(score, keys))


def pair_back(queries, slopes, statistics, keys, values, bias):
    scores = dot_t(jnp.concatenate([queries, statistics], 1), keys) * 0.125 + bias
    attention = jnp.exp(scores)
    prob = dot_t(jnp.concatenate([slopes, statistics], 1), values)
    score = (attention * prob * 0.125).astype(BF16)
    return merge_heads(t_dot(score, queries)), merge_heads(t_dot(attention.astype(BF16), slopes))


def put_head_columns(total, pair, column):
    head = lax.broadcasted_iota(jnp.int32, total.shape, 1) // 8
    total = jnp.where(head == 2 * pair, column[:UNIT], total)
    return jnp.where(head == 2 * pair + 1, column[UNIT:], total)


def statistics_of(lse, slope, mixed, heads):
    product = slope.astype(F32) * mixed
    high = product.astype(BF16)
    low = (product - high.astype(F32)).astype(BF16)
    mean = dot(high, heads) + dot(low, heads)
    lane = lax.broadcasted_iota(jnp.int32, lse.shape, 1)
    part = lane % 8
    value = jnp.where(part < 3, lse * -8.0, -mean)
    first = value.astype(BF16)
    rest = value - first.astype(F32)
    second = rest.astype(BF16)
    third = rest - second.astype(F32)
    value = jnp.where(part % 3 == 0, first.astype(F32), jnp.where(part % 3 == 1, second.astype(F32), third))
    return jnp.where((part < 6) & (lane < 64), value, 0.0).astype(BF16)


def norm(field, gain):
    factor = lax.rsqrt(jnp.mean(field * field, axis=-1, keepdims=True) + EPSILON)
    normed = field * factor
    return factor, normed, (normed * gain).astype(BF16)


def input_back(slope, hidden_slope, field, gain):
    factor = lax.rsqrt(jnp.mean(field * field, axis=-1, keepdims=True) + EPSILON)
    normed = field * factor
    scaled = hidden_slope * gain
    return slope + factor * (scaled - normed * jnp.mean(scaled * normed, axis=-1, keepdims=True))


class Reducer:
    def __init__(self, lay, place, wires, refs):
        self.lay, self.place, self.wires = lay, place, wires
        (
            self.given, self.in_1a, self.in_1b, self.sum_2a, self.sum_2b,
            self.in_2a, self.in_2b, self.sum_3, self.in_3, self.full,
        ) = refs
        self.copies = []

    def device(self, core=None, y=None, x=None, z=None):
        here = self.place
        core = here["core"] if core is None else core
        y = here["y"] if y is None else y
        x = here["x"] if x is None else x
        z = here["z"] if z is None else z
        return (y % self.lay.sec, y // self.lay.sec * 2 + core, x * self.lay.z + z)

    def send(self, source, target, device):
        copy = self.wires(source, target, device)
        copy.start()
        self.copies.append(copy)

    def arrive(self):
        for copy in self.copies:
            copy.wait()
        self.copies = []

    def first_start(self):
        lay, here = self.lay, self.place
        low = pl.ds(0, lay.z_low)
        high = pl.ds(lay.z_low, lay.z - lay.z_low)
        for step in range(1, lay.x):
            x = (here["x"] + step) % lay.x
            self.send(self.given.at[:, x, low], self.in_1a.at[step - 1], self.device(x=x))
        for step in range(1, lay.y):
            y = (here["y"] + step) % lay.y
            self.send(self.given.at[y, :, high], self.in_1b.at[step - 1], self.device(y=y))

    def first_finish(self):
        self.arrive()
        lay, here = self.lay, self.place
        low = pl.ds(0, lay.z_low)
        high = pl.ds(lay.z_low, lay.z - lay.z_low)

        @pl.loop(0, lay.y)
        def _(y):
            total = self.given[y, here["x"], low].astype(F32)
            for k in range(lay.x - 1):
                total += self.in_1a[k, y].astype(F32)
            self.sum_2a[y] = total.astype(BF16)

        @pl.loop(0, lay.x)
        def _(x):
            total = self.given[here["y"], x, high].astype(F32)
            for k in range(lay.y - 1):
                total += self.in_1b[k, x].astype(F32)
            self.sum_2b[x] = total.astype(BF16)

    def second_start(self):
        lay, here = self.lay, self.place
        for step in range(1, lay.y):
            y = (here["y"] + step) % lay.y
            self.send(self.sum_2a.at[y], self.in_2a.at[step - 1], self.device(y=y))
        for step in range(1, lay.x):
            x = (here["x"] + step) % lay.x
            self.send(self.sum_2b.at[x], self.in_2b.at[step - 1], self.device(x=x))

    def second_finish(self):
        self.arrive()
        lay, here = self.lay, self.place
        total = self.sum_2a[here["y"]].astype(F32)
        for k in range(lay.y - 1):
            total += self.in_2a[k].astype(F32)
        self.sum_3[pl.ds(0, lay.z_low)] = total.astype(BF16)
        total = self.sum_2b[here["x"]].astype(F32)
        for k in range(lay.x - 1):
            total += self.in_2b[k].astype(F32)
        self.sum_3[pl.ds(lay.z_low, lay.z - lay.z_low)] = total.astype(BF16)

    def third_start(self):
        lay, here = self.lay, self.place
        for step in range(1, lay.z):
            z = (here["z"] + step) % lay.z
            self.send(self.sum_3.at[z], self.in_3.at[step - 1], self.device(z=z))

    def third_finish(self):
        self.arrive()
        lay, here = self.lay, self.place
        total = self.sum_3[here["z"]].astype(F32)
        for k in range(lay.z - 1):
            total += self.in_3[k].astype(F32)
        self.full[here["core"], here["y"]] = total.astype(BF16)

    def last_start(self):
        lay, here = self.lay, self.place
        own = self.full.at[here["core"], here["y"]]
        for across in range(2):
            for step in range(lay.y):
                if across or step:
                    core = (here["core"] + across) % 2
                    y = (here["y"] + step) % lay.y
                    self.send(own, own, self.device(core=core, y=y))

    def last_finish(self):
        self.arrive()

    def column(self, start, width):
        size = self.full.shape[-1]
        parts = []
        while width > 0:
            group, offset = divmod(start, size)
            take = min(width, size - offset)
            parts.append(self.full[group // self.lay.y, group % self.lay.y, :, offset : offset + take])
            start, width = start + take, width - take
        return (parts[0] if len(parts) == 1 else jnp.concatenate(parts, 1)).astype(F32)

    def put(self, start, product):
        lay = self.lay
        size = self.given.shape[-1]
        done, width = 0, product.shape[1]
        while done < width:
            group, offset = divmod(start + done, size)
            take = min(width - done, size - offset)
            piece = product[:, done : done + take].astype(BF16)
            self.given[group, :, :, :, offset : offset + take] = piece.reshape(lay.x, lay.z, lay.depth, take)
            done += take

    def put_merged(self, part, product):
        lay = self.lay
        size = self.given.shape[-1]
        count = lay.blocks // 4
        shaped = product.astype(BF16).reshape(count, 4, lay.depth, D)
        for run in range(4):
            group, offset = divmod(run * D, size)
            for block in range(count):
                x, z = divmod(part * count + block, lay.z)
                self.given[group, x, z, :, offset : offset + D] = shaped[block, run]


def gain_back(lay, lon, total, weight, gain):
    own = weight[pl.ds(pl.multiple_of(lon * lay.depth, lay.depth), lay.depth), :].astype(F32)
    column = jnp.sum(total * own, axis=1, keepdims=True)
    row = lax.broadcasted_iota(jnp.int32, (lay.depth, D), 0) + lon * lay.depth
    at = lax.broadcasted_iota(jnp.int32, (lay.depth, D), 1) == row
    column = column / jnp.sum(jnp.where(at, gain, 0.0), axis=1, keepdims=True)
    square = (lay.depth, lay.depth)
    same = lax.broadcasted_iota(jnp.int32, square, 0) == lax.broadcasted_iota(jnp.int32, square, 1)
    return jnp.sum(jnp.where(same, column, 0.0), axis=0, keepdims=True)


def kernel(
    lay,
    tokens, cotangent, fine_gain, coarse_gain, bias_ref, bias_back_ref, heads_ref, columns_ref, merge_ref, split_ref,
    fine_attend_hbm, fine_output_hbm, merge_hbm, coarse_attend_hbm, coarse_output_hbm,
    coarse_field, token_gradient, fine_gain_out, coarse_gain_out, coarse_full, early_full, late_full,
    fine_attend, fine_output, merge_weight, coarse_attend, coarse_output,
    strip, field_f, wide_f, projected_f, attention_f, exact_f, lse_f, slope_wide_f, left_f, right_f, merged,
    field_c, wide_c, slope_wide_c, projected_c, mixed_slope_c, attention_c, exact_c, lse_c, statistics_c, factors_c,
    *rest,
):
    load_sem, send_sem, recv_sem = rest[30:]
    sec, lat, lon = (lax.axis_index(k) for k in ("sec", "lat", "lon"))
    core = lat % 2
    place = {"core": core, "y": lat // 2 * lay.sec + sec, "x": lon // lay.z, "z": lon % lay.z}
    used = [0]

    def wires(source, target, device):
        index = used[0]
        used[0] += 1
        return pltpu.make_async_remote_copy(
            src_ref=source,
            dst_ref=target,
            send_sem=send_sem.at[index],
            recv_sem=recv_sem.at[index],
            device_id=device,
            device_id_type=MESH,
        )

    def neighbour(step):
        return (sec, (lat + step[0] + lay.lat) % lay.lat, (lon + step[1] + lay.lon) % lay.lon)

    def start_rims(source, target):
        copies = []
        for step in AROUND:
            copy = wires(source(step), target(step), neighbour(step))
            if step[0]:
                last = lay.lat - 1
                sends = lat != (last if step[0] > 0 else 0)
                takes = lat != (0 if step[0] > 0 else last)
                pl.when(sends)(copy.start)
                copies.append((copy, sends, takes))
            else:
                copy.start()
                copies.append((copy, None, None))
        return copies

    def wait_rims(copies):
        for copy, sends, takes in copies:
            if sends is None:
                copy.wait()
            else:
                pl.when(sends)(copy.wait_send)
                pl.when(takes)(copy.wait_recv)

    def start_twin(source, target):
        copy = wires(source, target, coarse_sum.device(core=1 - core))
        copy.start()
        return copy

    coarse_sum = Reducer(lay, place, wires, rest[:10])
    early_sum = Reducer(lay, place, wires, rest[10:20])
    late_sum = Reducer(lay, place, wires, rest[20:30])

    loads = [
        pltpu.make_async_copy(source, target, load_sem.at[i])
        for i, (source, target) in enumerate(
            (
                (fine_attend_hbm, fine_attend),
                (fine_output_hbm, fine_output),
                (merge_hbm, merge_weight),
                (coarse_attend_hbm, coarse_attend),
                (coarse_output_hbm, coarse_output),
            )
        )
    ]
    for load in loads:
        load.start()

    for ref in (wide_f, slope_wide_f, wide_c, slope_wide_c, statistics_c):
        for row in (0, ref.shape[0] - 1):
            ref[row] = jnp.zeros(ref.shape[1:], ref.dtype)

    barrier = pltpu.get_barrier_semaphore()
    peers = [neighbour(step) for step in AROUND]
    peers += [coarse_sum.device(x=(place["x"] + s) % lay.x) for s in range(1, lay.x)]
    peers += [coarse_sum.device(z=(place["z"] + s) % lay.z) for s in range(1, lay.z)]
    peers += [
        coarse_sum.device(core=(core + c) % 2, y=(place["y"] + s) % lay.y)
        for c in range(2)
        for s in range(lay.y)
        if c or s
    ]
    for peer in peers:
        pl.semaphore_signal(barrier, inc=1, device_id=peer, device_id_type=MESH)

    field_f[...] = jnp.zeros_like(field_f)
    field_c[...] = jnp.zeros_like(field_c)
    for row in range(12):
        strip[row, :12] = tokens[0, row].astype(F32)
    for row in range(12):
        for half in range(2):
            start = (row // 6 * 2 + half) * UNIT + row % 6 * 8
            field_f[start : start + 6] = strip[row, 6 * half : 6 * half + 6]
    for unit in range(4):
        wide_f[1 + unit // 2, 1 + unit % 2] = field_f[unit * UNIT : (unit + 1) * UNIT].astype(BF16)
    for row in range(6):
        field_c[row * 8 : row * 8 + 6] = cotangent[0, row].astype(F32)
    slope_wide_c[1, 1] = field_c[...].astype(BF16)
    factors_c[5, 0] = field_c[...].astype(BF16)

    pl.semaphore_wait(barrier, len(peers))

    def part(step, mine):
        index = []
        for way in step:
            if way == 0:
                index.append(pl.ds(1, 2))
            elif way > 0:
                index.append(2 if mine else 3)
            else:
                index.append(1 if mine else 0)
        return tuple(index)

    def opposite(step):
        return (-step[0], -step[1])

    def fine_rims(ref):
        return start_rims(lambda step: ref.at[part(step, True)], lambda step: ref.at[part(opposite(step), False)])

    def coarse_rims(ref):
        return start_rims(lambda step: ref.at[1, 1], lambda step: ref.at[1 - step[0], 1 - step[1]])

    rims = fine_rims(wide_f)
    slope_rims = coarse_rims(slope_wide_c)

    top = jnp.where(lat == 0, NEGATIVE, 0.0)
    bottom = jnp.where(lat == lay.lat - 1, NEGATIVE, 0.0)
    lanes = lax.broadcasted_iota(jnp.int32, (1, 9 * UNIT), 1)

    def bias_at(is_first, is_last):
        above = jnp.where(is_first, top, 0.0)
        below = jnp.where(is_last, bottom, 0.0)
        rim = jnp.where(lanes < 3 * UNIT, above, 0.0) + jnp.where(lanes >= 6 * UNIT, below, 0.0)
        return bias_ref[...] + rim

    gain_f = fine_gain[...]
    gain_c = coarse_gain[...]
    loads[0].wait()
    for run in range(2):
        hidden = norm(field_f[run * 96 : run * 96 + 96], gain_f)[2]
        left_f[0, 0, run * 96 : run * 96 + 96] = hidden
        projected_f[240 + run * 192 : 336 + run * 192, :] = dot(hidden, fine_attend[...]).astype(BF16)
    twin_hidden = start_twin(left_f.at[0, 0], left_f.at[0, 1])
    wait_rims(rims)
    for start, units in (
        (0, (wide_f[0].reshape(4 * UNIT, D), wide_f[1, 0])),
        (336, (wide_f[1, 3], wide_f[2, 0])),
        (528, (wide_f[2, 3], wide_f[3].reshape(4 * UNIT, D))),
    ):
        field = jnp.concatenate([unit.astype(F32) for unit in units], 0)
        hidden = norm(field, gain_f)[2]
        projected_f[start : start + field.shape[0], :] = dot(hidden, fine_attend[...]).astype(BF16)

    def starts_of(quad):
        first, second = quad // 2, quad % 2
        return [pl.multiple_of(((first + i) * 4 + second) * UNIT, UNIT) for i in range(3)]

    def middle_of(quad):
        return pl.ds(pl.multiple_of(((1 + quad // 2) * 4 + 1 + quad % 2) * UNIT, UNIT), UNIT)

    def own_of(quad):
        return pl.ds(pl.multiple_of(quad * UNIT, UNIT), UNIT)

    @pl.loop(0, 4)
    def _(quad):
        first = quad // 2
        own, middle, starts = own_of(quad), middle_of(quad), starts_of(quad)
        bias = bias_at(first == 0, first == 1)
        lse = jnp.zeros((UNIT, 128), F32)
        for pair in range(PAIRS):
            low, high = pair * 128, pair * 128 + 128
            query = stack_heads(projected_f[middle, low:high])
            keys = unit_window(3 * UNIT, starts, projected_f, D + low)
            values = unit_window(3 * UNIT, starts, projected_f, 2 * D + low)
            attention, mixed, column = attend(query, keys, values, bias)
            attention_f[quad, pair] = attention
            exact_f[own, low:high] = mixed
            left_f[1, 0, own, low:high] = mixed.astype(BF16)
            lse = put_head_columns(lse, pair, column)
        lse_f[own, :] = lse

    twin_mixed = start_twin(left_f.at[1, 0], left_f.at[1, 1])
    loads[1].wait()
    fine_field = (field_f[...] + dot(left_f[1, 0], fine_output[...])).astype(BF16)
    merged[0] = dot(merge_ref[...], fine_field).astype(BF16)
    loads[2].wait()
    coarse_in = jnp.zeros((UNIT, D), F32)
    for quarter in range(4):
        rows = slice(quarter * UNIT, (quarter + 1) * UNIT)
        coarse_in += dot(merged[0, rows], merge_weight[quarter * D : (quarter + 1) * D])
    wide_c[1, 1] = coarse_in.astype(BF16)
    rims = coarse_rims(wide_c)
    twin_merged = start_twin(merged.at[0], merged.at[1])

    loads[3].wait()
    loads[4].wait()
    field_c[...] = wide_c[1, 1].astype(F32)
    factors_c[0, 0] = norm(field_c[...], gain_c)[2]
    wait_rims(slope_rims)
    mixed_slope_c[...] = dot_t(slope_wide_c[...].reshape(9 * UNIT, D), coarse_output[...]).astype(BF16)
    wait_rims(rims)
    hidden = norm(wide_c[...].reshape(9 * UNIT, D).astype(F32), gain_c)[2]
    projected_c[...] = dot(hidden, coarse_attend[...]).astype(BF16)
    bias = bias_at(True, True)
    middle = slice(4 * UNIT, 5 * UNIT)
    lse = jnp.zeros((UNIT, 128), F32)
    for pair in range(PAIRS):
        low, high = pair * 128, pair * 128 + 128
        query = stack_heads(projected_c[middle, low:high])
        keys, values = projected_c[:, D + low : D + high], projected_c[:, 2 * D + low : 2 * D + high]
        attention, mixed, column = attend(query, keys, values, bias)
        attention_c[pair] = attention
        exact_c[:, low:high] = mixed
        lse = put_head_columns(lse, pair, column)
    statistics_c[1, 1] = statistics_of(lse, mixed_slope_c[middle, :], exact_c[...], heads_ref[...])
    rims = coarse_rims(statistics_c)
    factors_c[4, 0] = exact_c[...].astype(BF16)
    moved = field_c[...] + dot(factors_c[4, 0], coarse_output[...])
    for row in range(6):
        coarse_field[0, row] = moved[row * 8 : row * 8 + 6].astype(BF16)
    for pair in range(PAIRS):
        low, high = pair * 128, pair * 128 + 128
        keys, values = projected_c[:, D + low : D + high], projected_c[:, 2 * D + low : 2 * D + high]
        slope = stack_heads(mixed_slope_c[middle, low:high])
        factors_c[1, 0, :, low:high] = query_back(keys, values, attention_c[pair], slope).astype(BF16)
    wait_rims(rims)
    statistics = statistics_c[...].reshape(9 * UNIT, 128)
    for pair in range(PAIRS):
        low, high = pair * 128, pair * 128 + 128
        keys = jnp.concatenate([stack_heads(projected_c[middle, D + low : D + high]), columns_ref[0, pair]], 1)
        values = jnp.concatenate(
            [stack_heads(projected_c[middle, 2 * D + low : 2 * D + high]), columns_ref[1, pair]], 1
        )
        key_slope, value_slope = pair_back(
            projected_c[:, low:high], mixed_slope_c[:, low:high], statistics, keys, values, bias_back_ref[...]
        )
        factors_c[2, 0, :, low:high] = key_slope.astype(BF16)
        factors_c[3, 0, :, low:high] = value_slope.astype(BF16)
    hidden_slope = sum(
        dot_t(factors_c[1 + k, 0], coarse_attend[:, k * D : (k + 1) * D]) for k in range(3)
    )
    slope = factors_c[5, 0].astype(F32)
    coarse_slope = input_back(slope, hidden_slope, field_c[...], gain_c).astype(BF16)
    factors_c[6, 0] = coarse_slope
    twin_factors = start_twin(factors_c.at[:, 0], factors_c.at[:, 1])

    merged_slope = jnp.concatenate(
        [dot_t(coarse_slope, merge_weight[k * D : (k + 1) * D]).astype(BF16) for k in range(4)], 0
    )
    slope_f = dot(split_ref[...], merged_slope).astype(BF16)
    right_f[1, 0] = slope_f
    mixed_slope = dot_t(slope_f, fine_output[...]).astype(BF16)
    statistics = statistics_of(lse_f[...], mixed_slope, exact_f[...], heads_ref[...])
    for unit in range(4):
        rows = slice(unit * UNIT, (unit + 1) * UNIT)
        slope_wide_f[1 + unit // 2, 1 + unit % 2, :, :D] = mixed_slope[rows]
        slope_wide_f[1 + unit // 2, 1 + unit % 2, :, D:] = statistics[rows]
    rims = fine_rims(slope_wide_f)
    twin_slope = start_twin(right_f.at[1, 0], right_f.at[1, 1])

    twin_factors.wait()
    twin_merged.wait()

    def both(index):
        return factors_c[index].reshape(2 * UNIT, D)

    @pl.when(core == 0)
    def _():
        for k in range(3):
            coarse_sum.put(k * D, t_dot(both(0), both(1 + k)))
        coarse_sum.put(3 * D, t_dot(both(4), both(5)))

    @pl.when(core == 1)
    def _():
        for k in range(4):
            rows = slice(k * UNIT, (k + 1) * UNIT)
            coarse_sum.put_merged(k, t_dot(merged[:, rows].reshape(2 * UNIT, D), both(6)))

    @pl.loop(0, 4)
    def _(quad):
        own, starts = own_of(quad), starts_of(quad)
        for pair in range(PAIRS):
            low, high = pair * 128, pair * 128 + 128
            slope = stack_heads(slope_wide_f[1 + quad // 2, 1 + quad % 2, :, low:high])
            keys = unit_window(3 * UNIT, starts, projected_f, D + low)
            values = unit_window(3 * UNIT, starts, projected_f, 2 * D + low)
            query_slope = query_back(keys, values, attention_f[quad, pair], slope)
            right_f[0, 0, own, low:high] = query_slope.astype(BF16)

    twin_query = start_twin(right_f.at[0, 0], right_f.at[0, 1])
    coarse_sum.first_start()
    twin_hidden.wait()
    twin_mixed.wait()
    twin_slope.wait()
    twin_query.wait()
    early_sum.put(0, t_dot(left_f[core].reshape(8 * UNIT, D), right_f[core].reshape(8 * UNIT, D)))
    wait_rims(rims)
    early_sum.first_start()

    @pl.loop(0, 4)
    def _(quad):
        own, middle, starts = own_of(quad), middle_of(quad), starts_of(quad)
        first, second = quad // 2, quad % 2

        def around(low, high):
            rows = [slope_wide_f[first + i, pl.ds(second, 3), :, low:high] for i in range(3)]
            return jnp.concatenate([r.reshape(3 * UNIT, high - low) for r in rows], 0)

        statistics = around(D, D + 128)
        for pair in range(PAIRS):
            low, high = pair * 128, pair * 128 + 128
            keys = jnp.concatenate([stack_heads(projected_f[middle, D + low : D + high]), columns_ref[0, pair]], 1)
            values = jnp.concatenate(
                [stack_heads(projected_f[middle, 2 * D + low : 2 * D + high]), columns_ref[1, pair]], 1
            )
            key_slope, value_slope = pair_back(
                unit_window(3 * UNIT, starts, projected_f, low),
                around(low, high),
                statistics,
                keys,
                values,
                bias_back_ref[...],
            )
            right_f[2, 0, own, low:high] = key_slope.astype(BF16)
            right_f[3, 0, own, low:high] = value_slope.astype(BF16)

    other = 3 - core
    twin_pair = start_twin(right_f.at[other, 0], right_f.at[other, 1])
    hidden_slope = dot_t(right_f[0, 0], fine_attend[:, :D])
    hidden_slope += dot_t(right_f[2, 0], fine_attend[:, D : 2 * D])
    hidden_slope += dot_t(right_f[3, 0], fine_attend[:, 2 * D :])
    twin_pair.wait()
    late_sum.put(0, t_dot(left_f[0].reshape(8 * UNIT, D), right_f[2 + core].reshape(8 * UNIT, D)))
    late_sum.first_start()
    coarse_sum.first_finish()
    coarse_sum.second_start()
    early_sum.first_finish()
    early_sum.second_start()
    slope = input_back(right_f[1, 0].astype(F32), hidden_slope, field_f[...], gain_f)
    for row in range(12):
        for half in range(2):
            start = (row // 6 * 2 + half) * UNIT + row % 6 * 8
            strip[row, 6 * half : 6 * half + 6] = slope[start : start + 6]
    for row in range(12):
        token_gradient[0, row] = strip[row, :12].astype(BF16)
    late_sum.first_finish()
    late_sum.second_start()
    coarse_sum.second_finish()
    coarse_sum.third_start()
    early_sum.second_finish()
    early_sum.third_start()
    late_sum.second_finish()
    late_sum.third_start()
    coarse_sum.third_finish()
    coarse_sum.last_start()
    early_sum.third_finish()
    early_sum.last_start()
    late_sum.third_finish()
    late_sum.last_start()
    coarse_sum.last_finish()
    coarse_full[...] = coarse_sum.full[...]
    coarse_gain_out[...] = gain_back(lay, lon, coarse_sum.column(0, 3 * D), coarse_attend, gain_c)
    early_sum.last_finish()
    early_full[...] = early_sum.full[...]
    late_sum.last_finish()
    late_full[...] = late_sum.full[...]
    total = jnp.concatenate([early_sum.column(0, D), late_sum.column(0, 2 * D)], 1)
    fine_gain_out[...] = gain_back(lay, lon, total, fine_attend, gain_f)


def finish(lay, *refs):
    field, gradient, fine_gain, coarse_gain, coarse_full, early_full, late_full = refs[:7]
    (
        field_out, gradient_out, fine_gain_out, fine_attend, fine_output, merge,
        coarse_gain_out, coarse_attend, coarse_output,
    ) = refs[7:]
    field_out[...] = field[...]
    gradient_out[...] = gradient[...]
    fine_gain_out[...] = fine_gain[...]
    coarse_gain_out[...] = coarse_gain[...]

    def column(full, start, width):
        return Reducer(lay, None, None, (None,) * 9 + (full,)).column(start, width)

    for k in range(3):
        fine_attend[:, k * D : (k + 1) * D] = column(late_full, (k - 1) * D, D) if k else column(early_full, 0, D)
        coarse_attend[:, k * D : (k + 1) * D] = column(coarse_full, k * D, D)
    fine_output[...] = column(early_full, D, D)
    coarse_output[...] = column(coarse_full, 3 * D, D)
    for run in range(4):
        merge[run * lay.depth : (run + 1) * lay.depth, :] = column(coarse_full, (4 + run) * D, D)


def reducer_scratch(lay, width):
    y, x, z, low = lay.y, lay.x, lay.z, lay.z_low
    high = z - low
    end = (lay.depth, width)
    shapes = (
        (y, x, z), (x - 1, y, low), (y - 1, x, high), (y, low), (x, high),
        (y - 1, low), (x - 1, high), (z,), (z - 1,), (2, y),
    )
    return [pltpu.VMEM(shape + end, BF16) for shape in shapes]


def per_device(
    lay,
    tokens,
    cotangent,
    fine_gain,
    fine_attend,
    fine_output,
    merge_weight,
    coarse_gain,
    coarse_attend,
    coarse_output,
):
    vmem = pl.BlockSpec(memory_space=pltpu.VMEM)
    hbm = pl.BlockSpec(memory_space=pl.ANY)
    select = merge_matrix()
    per_batch = 2 * (lay.x - 1 + lay.y - 1) + lay.z - 1 + 2 * lay.y - 1
    copies = 5 * 8 + 7 + 3 * per_batch
    depth = lay.depth
    fine_shape = jax.ShapeDtypeStruct((2, lay.y, depth, lay.fine_width), BF16)
    between = pl.pallas_call(
        functools.partial(kernel, lay),
        out_shape=(
            jax.ShapeDtypeStruct(cotangent.shape, BF16),
            jax.ShapeDtypeStruct(tokens.shape, BF16),
            jax.ShapeDtypeStruct((1, depth), F32),
            jax.ShapeDtypeStruct((1, depth), F32),
            jax.ShapeDtypeStruct((2, lay.y, depth, lay.coarse_width), BF16),
            fine_shape,
            fine_shape,
        ),
        in_specs=[vmem] * 10 + [hbm] * 5,
        out_specs=[vmem] * 7,
        scratch_shapes=[
            pltpu.VMEM((D, 3 * D), BF16),
            pltpu.VMEM((D, D), BF16),
            pltpu.VMEM((4 * D, D), BF16),
            pltpu.VMEM((D, 3 * D), BF16),
            pltpu.VMEM((D, D), BF16),
            pltpu.VMEM((12, 16, D), F32),
            pltpu.VMEM((4 * UNIT, D), F32),
            pltpu.VMEM((4, 4, UNIT, D), BF16),
            pltpu.VMEM((16 * UNIT, 3 * D), BF16),
            pltpu.VMEM((4, PAIRS, 2 * UNIT, 9 * UNIT), F32),
            pltpu.VMEM((4 * UNIT, D), F32),
            pltpu.VMEM((4 * UNIT, 128), F32),
            pltpu.VMEM((4, 4, UNIT, D + 128), BF16),
            pltpu.VMEM((2, 2, 4 * UNIT, D), BF16),
            pltpu.VMEM((4, 2, 4 * UNIT, D), BF16),
            pltpu.VMEM((2, 4 * UNIT, D), BF16),
            pltpu.VMEM((UNIT, D), F32),
            pltpu.VMEM((3, 3, UNIT, D), BF16),
            pltpu.VMEM((3, 3, UNIT, D), BF16),
            pltpu.VMEM((9 * UNIT, 3 * D), BF16),
            pltpu.VMEM((9 * UNIT, D), BF16),
            pltpu.VMEM((PAIRS, 2 * UNIT, 9 * UNIT), F32),
            pltpu.VMEM((UNIT, D), F32),
            pltpu.VMEM((UNIT, 128), F32),
            pltpu.VMEM((3, 3, UNIT, 128), BF16),
            pltpu.VMEM((7, 2, UNIT, D), BF16),
            *reducer_scratch(lay, lay.coarse_width),
            *reducer_scratch(lay, lay.fine_width),
            *reducer_scratch(lay, lay.fine_width),
            pltpu.SemaphoreType.DMA((5,)),
            pltpu.SemaphoreType.DMA((copies,)),
            pltpu.SemaphoreType.DMA((copies,)),
        ],
        compiler_params=pltpu.CompilerParams(
            collective_id=0, has_side_effects=True, vmem_limit_bytes=56 * 1024 * 1024
        ),
    )(
        tokens,
        cotangent,
        fine_gain.reshape(1, D),
        coarse_gain.reshape(1, D),
        jnp.asarray(window_bias()),
        jnp.asarray(window_bias_back()),
        jnp.asarray(head_columns(), BF16),
        jnp.asarray(statistic_columns(), BF16),
        jnp.asarray(select, BF16),
        jnp.asarray(select.T, BF16),
        fine_attend,
        fine_output,
        merge_weight,
        coarse_attend,
        coarse_output,
    )
    outs = pl.pallas_call(
        functools.partial(finish, lay),
        out_shape=(
            jax.ShapeDtypeStruct(cotangent.shape, BF16),
            jax.ShapeDtypeStruct(tokens.shape, BF16),
            jax.ShapeDtypeStruct((1, depth), F32),
            jax.ShapeDtypeStruct((depth, 3 * D), F32),
            jax.ShapeDtypeStruct((depth, D), F32),
            jax.ShapeDtypeStruct((4 * depth, D), F32),
            jax.ShapeDtypeStruct((1, depth), F32),
            jax.ShapeDtypeStruct((depth, 3 * D), F32),
            jax.ShapeDtypeStruct((depth, D), F32),
        ),
        in_specs=[vmem] * 7,
        out_specs=[vmem] * 9,
    )(*between)
    outs = list(outs)
    outs[2] = outs[2].reshape(depth)
    outs[6] = outs[6].reshape(depth)
    return tuple(outs)


def solution(mesh):
    return jax.shard_map(
        functools.partial(per_device, Layout(mesh)),
        mesh=mesh,
        in_specs=(
            P("sec", "lat", "lon", None),
            P("sec", "lat", "lon", None),
            P(),
            P(),
            P(),
            P(),
            P(),
            P(),
            P(),
        ),
        out_specs=(
            P("sec", "lat", "lon", None),
            P("sec", "lat", "lon", None),
            P("lon"),
            P("lon", None),
            P("lon", None),
            P("lon", None),
            P("lon"),
            P("lon", None),
            P("lon", None),
        ),
        check_vma=False,
    )
```

time: 127 us -> 92 us (0.72)
  Pallas kernels: 113 us -> 91.1 us
  local copies, waits for them, and re-layouts: 12.7 us -> 0 us
    pallas_call x1, Pallas kernels: 113 us -> 89.2 us  [per_device(): pl.pallas_call(functools.partial(kernel, lay), out_shape=(jax.ShapeDtypeS...]
    unnamed x9 -> x0, local copies, waits for them, and re-layouts: 12.7 us -> none
    pallas_call x0 -> x1, Pallas kernels: none -> 1.9 us  [per_device(): pl.pallas_call(functools.partial(finish, lay), out_shape=(jax.ShapeDtypeS...]
where the time goes in v2:
time: 92 us; the launch traced here: 91.9 us
  Pallas kernels  91.1 us (99%)
    pallas_call x1, Pallas kernels, per_device(): pl.pallas_call(functools.partial(kernel, lay), out_shape=(jax.ShapeDtypeS...  89.2 us
    pallas_call x1, Pallas kernels, per_device(): pl.pallas_call(functools.partial(finish, lay), out_shape=(jax.ShapeDtypeS...  1.9 us

profile of v2, /device:TPU:1, one launch (start us, length us, event | category | flops | bytes accessed | tf_op | source)
XLA Modules:
  0.0 91.9 jit_solution(17675409742011086247)
XLA Ops:
  0.6 89.2 %shard_map.214 = (bf16[1,6,6,512]{3,2,1,0:T(8,128)(2,1)}, bf16[1,12,12,512]{3,2,1,0:T(8,128)(2,1)}, f32[1,16]{1,0:T(1,128)}, f32[1,16]{1,0:T(1,128)}, bf16[2,4,1...) custom-call(bf16[1,12,12,512]{3,2,1,0:T(8,128)(2,1)} %tokens.1, ...), custom_call_target="tpu_custom_call" | custom-call | tf_op jit(solution)/shard_map/pallas_call | solution.py:766
  89.9 1.9 %shard_map.215 = (bf16[1,6,6,512]{3,2,1,0:T(8,128)(2,1)}, bf16[1,12,12,512]{3,2,1,0:T(8,128)(2,1)}, f32[1,16]{1,0:T(1,128)}, f32[16,1536]{1,0:T(8,128)}, f32[16,...) custom-call(bf16[1,6,6,512]{3,2,1,0:T(8,128)(2,1)} %get-tuple-element.25.refs_0, ...), custom_call_target="tpu_custom_call" | custom-call | tf_op jit(solution)/shard_map/pallas_call | solution.py:833

commit v3 on v2

--- a/solution.py
+++ b/solution.py
@@ -73,7 +73,7 @@
         for head in range(HEADS):
             pair, side = divmod(head, 2)
             start = head * 8 + 3 * which
-            matrix[which, pair, side * UNIT : (side + 1) * UNIT, start : start + 3] = 1.0
+            matrix[which, pair, side * UNIT : (side + 1) * UNIT, start : start + 3] = 0.125
     return matrix
 
 
@@ -112,7 +112,7 @@
 
 
 def stack_heads(part):
-    part = part.astype(F32)
+    part = part.astype(F32) * 0.125
     low = low_lanes(UNIT)
     return jnp.concatenate([jnp.where(low, part, 0.0), jnp.where(low, 0.0, part)], 0).astype(BF16)
 
@@ -121,28 +121,32 @@
     return jnp.where(low_lanes(UNIT), both[:UNIT], both[UNIT:])
 
 
-def attend(query, keys, values, bias):
-    scores = dot_t(query, keys) * 0.125 + bias
-    peak = jnp.max(scores, axis=-1, keepdims=True)
-    expo = jnp.exp(scores - peak)
-    total = jnp.sum(expo, axis=-1, keepdims=True)
-    attention = expo / total
-    return attention, merge_heads(dot(attention.astype(BF16), values)), peak + jnp.log(total)
-
-
-def query_back(keys, values, attention, slope):
-    prob = dot_t(slope, values)
-    mean = jnp.sum(attention * prob, axis=-1, keepdims=True)
-    score = (attention * (prob - mean) * 0.125).astype(BF16)
-    return merge_heads(dot(score, keys))
+def attend(queries, keys, values, bias):
+    scores = [dot_t(q, k) + bias for q, k in zip(queries, keys)]
+    peaks = [jnp.max(s, axis=-1, keepdims=True) for s in scores]
+    expos = [jnp.exp(s - m) for s, m in zip(scores, peaks)]
+    totals = [jnp.sum(e, axis=-1, keepdims=True) for e in expos]
+    attentions = [e * (1.0 / t) for e, t in zip(expos, totals)]
+    mixed = [merge_heads(dot(a.astype(BF16), v)) for a, v in zip(attentions, values)]
+    return attentions, mixed, [m + jnp.log(t) for m, t in zip(peaks, totals)]
+
+
+def query_back(keys, values, attentions, slopes):
+    probs = [dot_t(s, v) for s, v in zip(slopes, values)]
+    means = [jnp.sum(a * p, axis=-1, keepdims=True) for a, p in zip(attentions, probs)]
+    scores = [(a * (p - m)).astype(BF16) for a, p, m in zip(attentions, probs, means)]
+    return [merge_heads(dot(s, k)) for s, k in zip(scores, keys)]
 
 
 def pair_back(queries, slopes, statistics, keys, values, bias):
-    scores = dot_t(jnp.concatenate([queries, statistics], 1), keys) * 0.125 + bias
-    attention = jnp.exp(scores)
-    prob = dot_t(jnp.concatenate([slopes, statistics], 1), values)
-    score = (attention * prob * 0.125).astype(BF16)
-    return merge_heads(t_dot(score, queries)), merge_heads(t_dot(attention.astype(BF16), slopes))
+    scores = [dot_t(jnp.concatenate([q, statistics], 1), k) + bias for q, k in zip(queries, keys)]
+    probs = [dot_t(jnp.concatenate([s, statistics], 1), v) for s, v in zip(slopes, values)]
+    attentions = [jnp.exp(s) for s in scores]
+    scores = [(a * p).astype(BF16) for a, p in zip(attentions, probs)]
+    return (
+        [merge_heads(t_dot(s, q)) for s, q in zip(scores, queries)],
+        [merge_heads(t_dot(a.astype(BF16), s)) for a, s in zip(attentions, slopes)],
+    )
 
 
 def put_head_columns(total, pair, column):
@@ -319,6 +323,17 @@
                 self.given[group, x, z, :, offset : offset + D] = shaped[block, run]
 
 
+GROUPS = ((0, 1, 2, 3),)
+
+
+def lanes_of(pair, start=0):
+    return slice(start + pair * 128, start + pair * 128 + 128)
+
+
+def with_columns(part, columns):
+    return jnp.concatenate([stack_heads(part), columns], 1)
+
+
 def gain_back(lay, lon, total, weight, gain):
     own = weight[pl.ds(pl.multiple_of(lon * lay.depth, lay.depth), lay.depth), :].astype(F32)
     column = jnp.sum(total * own, axis=1, keepdims=True)
@@ -332,10 +347,12 @@
 
 def kernel(
     lay,
-    tokens, cotangent, fine_gain, coarse_gain, bias_ref, bias_back_ref, heads_ref, columns_ref, merge_ref, split_ref,
+    tokens, cotangent, fine_gain, coarse_gain,
     fine_attend_hbm, fine_output_hbm, merge_hbm, coarse_attend_hbm, coarse_output_hbm,
+    bias_hbm, bias_back_hbm, heads_hbm, columns_hbm, merge_ref_hbm, split_hbm,
     coarse_field, token_gradient, fine_gain_out, coarse_gain_out, coarse_full, early_full, late_full,
     fine_attend, fine_output, merge_weight, coarse_attend, coarse_output,
+    bias_ref, bias_back_ref, heads_ref, columns_ref, merge_ref, split_ref,
     strip, field_f, wide_f, projected_f, attention_f, exact_f, lse_f, slope_wide_f, left_f, right_f, merged,
     field_c, wide_c, slope_wide_c, projected_c, mixed_slope_c, attention_c, exact_c, lse_c, statistics_c, factors_c,
     *rest,
@@ -393,25 +410,6 @@
     early_sum = Reducer(lay, place, wires, rest[10:20])
     late_sum = Reducer(lay, place, wires, rest[20:30])
 
-    loads = [
-        pltpu.make_async_copy(source, target, load_sem.at[i])
-        for i, (source, target) in enumerate(
-            (
-                (fine_attend_hbm, fine_attend),
-                (fine_output_hbm, fine_output),
-                (merge_hbm, merge_weight),
-                (coarse_attend_hbm, coarse_attend),
-                (coarse_output_hbm, coarse_output),
-            )
-        )
-    ]
-    for load in loads:
-        load.start()
-
-    for ref in (wide_f, slope_wide_f, wide_c, slope_wide_c, statistics_c):
-        for row in (0, ref.shape[0] - 1):
-            ref[row] = jnp.zeros(ref.shape[1:], ref.dtype)
-
     barrier = pltpu.get_barrier_semaphore()
     peers = [neighbour(step) for step in AROUND]
     peers += [coarse_sum.device(x=(place["x"] + s) % lay.x) for s in range(1, lay.x)]
@@ -424,6 +422,27 @@
     ]
     for peer in peers:
         pl.semaphore_signal(barrier, inc=1, device_id=peer, device_id_type=MESH)
+
+    loads = {
+        name: pltpu.make_async_copy(source, target, load_sem.at[i])
+        for i, (name, source, target) in enumerate(
+            (
+                ("fine_attend", fine_attend_hbm, fine_attend),
+                ("bias_ref", bias_hbm, bias_ref),
+                ("fine_output", fine_output_hbm, fine_output),
+                ("merge_ref", merge_ref_hbm, merge_ref),
+                ("merge_weight", merge_hbm, merge_weight),
+                ("coarse_output", coarse_output_hbm, coarse_output),
+                ("coarse_attend", coarse_attend_hbm, coarse_attend),
+                ("heads_ref", heads_hbm, heads_ref),
+                ("columns_ref", columns_hbm, columns_ref),
+                ("bias_back_ref", bias_back_hbm, bias_back_ref),
+                ("split_ref", split_hbm, split_ref),
+            )
+        )
+    }
+    for load in loads.values():
+        load.start()
 
     field_f[...] = jnp.zeros_like(field_f)
     field_c[...] = jnp.zeros_like(field_c)
@@ -463,7 +482,13 @@
         return start_rims(lambda step: ref.at[1, 1], lambda step: ref.at[1 - step[0], 1 - step[1]])
 
     rims = fine_rims(wide_f)
-    slope_rims = coarse_rims(slope_wide_c)
+
+    def clear(row):
+        for ref in (wide_f, slope_wide_f, wide_c, slope_wide_c, statistics_c):
+            ref[row if row == 0 else ref.shape[0] - 1] = jnp.zeros(ref.shape[1:], ref.dtype)
+
+    pl.when(lat == 0)(lambda: clear(0))
+    pl.when(lat == lay.lat - 1)(lambda: clear(-1))
 
     top = jnp.where(lat == 0, NEGATIVE, 0.0)
     bottom = jnp.where(lat == lay.lat - 1, NEGATIVE, 0.0)
@@ -477,13 +502,14 @@
 
     gain_f = fine_gain[...]
     gain_c = coarse_gain[...]
-    loads[0].wait()
+    loads["fine_attend"].wait()
     for run in range(2):
         hidden = norm(field_f[run * 96 : run * 96 + 96], gain_f)[2]
         left_f[0, 0, run * 96 : run * 96 + 96] = hidden
         projected_f[240 + run * 192 : 336 + run * 192, :] = dot(hidden, fine_attend[...]).astype(BF16)
     twin_hidden = start_twin(left_f.at[0, 0], left_f.at[0, 1])
     wait_rims(rims)
+    slope_rims = coarse_rims(slope_wide_c)
     for start, units in (
         (0, (wide_f[0].reshape(4 * UNIT, D), wide_f[1, 0])),
         (336, (wide_f[1, 3], wide_f[2, 0])),
@@ -493,6 +519,8 @@
         hidden = norm(field, gain_f)[2]
         projected_f[start : start + field.shape[0], :] = dot(hidden, fine_attend[...]).astype(BF16)
 
+    loads["bias_ref"].wait()
+
     def starts_of(quad):
         first, second = quad // 2, quad % 2
         return [pl.multiple_of(((first + i) * 4 + second) * UNIT, UNIT) for i in range(3)]
@@ -509,23 +537,26 @@
         own, middle, starts = own_of(quad), middle_of(quad), starts_of(quad)
         bias = bias_at(first == 0, first == 1)
         lse = jnp.zeros((UNIT, 128), F32)
-        for pair in range(PAIRS):
-            low, high = pair * 128, pair * 128 + 128
-            query = stack_heads(projected_f[middle, low:high])
-            keys = unit_window(3 * UNIT, starts, projected_f, D + low)
-            values = unit_window(3 * UNIT, starts, projected_f, 2 * D + low)
-            attention, mixed, column = attend(query, keys, values, bias)
-            attention_f[quad, pair] = attention
-            exact_f[own, low:high] = mixed
-            left_f[1, 0, own, low:high] = mixed.astype(BF16)
-            lse = put_head_columns(lse, pair, column)
+        for pairs in GROUPS:
+            results = attend(
+                [stack_heads(projected_f[middle, lanes_of(pair)]) for pair in pairs],
+                [unit_window(3 * UNIT, starts, projected_f, D + pair * 128) for pair in pairs],
+                [unit_window(3 * UNIT, starts, projected_f, 2 * D + pair * 128) for pair in pairs],
+                bias,
+            )
+            for pair, attention, mixed, column in zip(pairs, *results):
+                attention_f[quad, pair] = attention
+                exact_f[own, lanes_of(pair)] = mixed
+                left_f[1, 0, own, lanes_of(pair)] = mixed.astype(BF16)
+                lse = put_head_columns(lse, pair, column)
         lse_f[own, :] = lse
 
     twin_mixed = start_twin(left_f.at[1, 0], left_f.at[1, 1])
-    loads[1].wait()
+    loads["fine_output"].wait()
+    loads["merge_ref"].wait()
     fine_field = (field_f[...] + dot(left_f[1, 0], fine_output[...])).astype(BF16)
     merged[0] = dot(merge_ref[...], fine_field).astype(BF16)
-    loads[2].wait()
+    loads["merge_weight"].wait()
     coarse_in = jnp.zeros((UNIT, D), F32)
     for quarter in range(4):
         rows = slice(quarter * UNIT, (quarter + 1) * UNIT)
@@ -534,8 +565,8 @@
     rims = coarse_rims(wide_c)
     twin_merged = start_twin(merged.at[0], merged.at[1])
 
-    loads[3].wait()
-    loads[4].wait()
+    for name in ("coarse_output", "coarse_attend", "heads_ref", "columns_ref", "bias_back_ref", "split_ref"):
+        loads[name].wait()
     field_c[...] = wide_c[1, 1].astype(F32)
     factors_c[0, 0] = norm(field_c[...], gain_c)[2]
     wait_rims(slope_rims)
@@ -546,38 +577,46 @@
     bias = bias_at(True, True)
     middle = slice(4 * UNIT, 5 * UNIT)
     lse = jnp.zeros((UNIT, 128), F32)
-    for pair in range(PAIRS):
-        low, high = pair * 128, pair * 128 + 128
-        query = stack_heads(projected_c[middle, low:high])
-        keys, values = projected_c[:, D + low : D + high], projected_c[:, 2 * D + low : 2 * D + high]
-        attention, mixed, column = attend(query, keys, values, bias)
-        attention_c[pair] = attention
-        exact_c[:, low:high] = mixed
-        lse = put_head_columns(lse, pair, column)
+    for pairs in GROUPS:
+        results = attend(
+            [stack_heads(projected_c[middle, lanes_of(pair)]) for pair in pairs],
+            [projected_c[:, lanes_of(pair, D)] for pair in pairs],
+            [projected_c[:, lanes_of(pair, 2 * D)] for pair in pairs],
+            bias,
+        )
+        for pair, attention, mixed, column in zip(pairs, *results):
+            attention_c[pair] = attention
+            exact_c[:, lanes_of(pair)] = mixed
+            lse = put_head_columns(lse, pair, column)
     statistics_c[1, 1] = statistics_of(lse, mixed_slope_c[middle, :], exact_c[...], heads_ref[...])
     rims = coarse_rims(statistics_c)
     factors_c[4, 0] = exact_c[...].astype(BF16)
     moved = field_c[...] + dot(factors_c[4, 0], coarse_output[...])
     for row in range(6):
         coarse_field[0, row] = moved[row * 8 : row * 8 + 6].astype(BF16)
-    for pair in range(PAIRS):
-        low, high = pair * 128, pair * 128 + 128
-        keys, values = projected_c[:, D + low : D + high], projected_c[:, 2 * D + low : 2 * D + high]
-        slope = stack_heads(mixed_slope_c[middle, low:high])
-        factors_c[1, 0, :, low:high] = query_back(keys, values, attention_c[pair], slope).astype(BF16)
+    for pairs in GROUPS:
+        results = query_back(
+            [projected_c[:, lanes_of(pair, D)] for pair in pairs],
+            [projected_c[:, lanes_of(pair, 2 * D)] for pair in pairs],
+            [attention_c[pair] for pair in pairs],
+            [stack_heads(mixed_slope_c[middle, lanes_of(pair)]) for pair in pairs],
+        )
+        for pair, query_slope in zip(pairs, results):
+            factors_c[1, 0, :, lanes_of(pair)] = query_slope.astype(BF16)
     wait_rims(rims)
     statistics = statistics_c[...].reshape(9 * UNIT, 128)
-    for pair in range(PAIRS):
-        low, high = pair * 128, pair * 128 + 128
-        keys = jnp.concatenate([stack_heads(projected_c[middle, D + low : D + high]), columns_ref[0, pair]], 1)
-        values = jnp.concatenate(
-            [stack_heads(projected_c[middle, 2 * D + low : 2 * D + high]), columns_ref[1, pair]], 1
+    for pairs in GROUPS:
+        results = pair_back(
+            [projected_c[:, lanes_of(pair)] for pair in pairs],
+            [mixed_slope_c[:, lanes_of(pair)] for pair in pairs],
+            statistics,
+            [with_columns(projected_c[middle, lanes_of(pair, D)], columns_ref[0, pair]) for pair in pairs],
+            [with_columns(projected_c[middle, lanes_of(pair, 2 * D)], columns_ref[1, pair]) for pair in pairs],
+            bias_back_ref[...],
         )
-        key_slope, value_slope = pair_back(
-            projected_c[:, low:high], mixed_slope_c[:, low:high], statistics, keys, values, bias_back_ref[...]
-        )
-        factors_c[2, 0, :, low:high] = key_slope.astype(BF16)
-        factors_c[3, 0, :, low:high] = value_slope.astype(BF16)
+        for pair, key_slope, value_slope in zip(pairs, *results):
+            factors_c[2, 0, :, lanes_of(pair)] = key_slope.astype(BF16)
+            factors_c[3, 0, :, lanes_of(pair)] = value_slope.astype(BF16)
     hidden_slope = sum(
         dot_t(factors_c[1 + k, 0], coarse_attend[:, k * D : (k + 1) * D]) for k in range(3)
     )
@@ -618,19 +657,22 @@
             rows = slice(k * UNIT, (k + 1) * UNIT)
             coarse_sum.put_merged(k, t_dot(merged[:, rows].reshape(2 * UNIT, D), both(6)))
 
+    coarse_sum.first_start()
+
     @pl.loop(0, 4)
     def _(quad):
         own, starts = own_of(quad), starts_of(quad)
-        for pair in range(PAIRS):
-            low, high = pair * 128, pair * 128 + 128
-            slope = stack_heads(slope_wide_f[1 + quad // 2, 1 + quad % 2, :, low:high])
-            keys = unit_window(3 * UNIT, starts, projected_f, D + low)
-            values = unit_window(3 * UNIT, starts, projected_f, 2 * D + low)
-            query_slope = query_back(keys, values, attention_f[quad, pair], slope)
-            right_f[0, 0, own, low:high] = query_slope.astype(BF16)
+        for pairs in GROUPS:
+            results = query_back(
+                [unit_window(3 * UNIT, starts, projected_f, D + pair * 128) for pair in pairs],
+                [unit_window(3 * UNIT, starts, projected_f, 2 * D + pair * 128) for pair in pairs],
+                [attention_f[quad, pair] for pair in pairs],
+                [stack_heads(slope_wide_f[1 + quad // 2, 1 + quad % 2, :, lanes_of(pair)]) for pair in pairs],
+            )
+            for pair, query_slope in zip(pairs, results):
+                right_f[0, 0, own, lanes_of(pair)] = query_slope.astype(BF16)
 
     twin_query = start_twin(right_f.at[0, 0], right_f.at[0, 1])
-    coarse_sum.first_start()
     twin_hidden.wait()
     twin_mixed.wait()
     twin_slope.wait()
@@ -644,27 +686,23 @@
         own, middle, starts = own_of(quad), middle_of(quad), starts_of(quad)
         first, second = quad // 2, quad % 2
 
-        def around(low, high):
-            rows = [slope_wide_f[first + i, pl.ds(second, 3), :, low:high] for i in range(3)]
-            return jnp.concatenate([r.reshape(3 * UNIT, high - low) for r in rows], 0)
-
-        statistics = around(D, D + 128)
-        for pair in range(PAIRS):
-            low, high = pair * 128, pair * 128 + 128
-            keys = jnp.concatenate([stack_heads(projected_f[middle, D + low : D + high]), columns_ref[0, pair]], 1)
-            values = jnp.concatenate(
-                [stack_heads(projected_f[middle, 2 * D + low : 2 * D + high]), columns_ref[1, pair]], 1
-            )
-            key_slope, value_slope = pair_back(
-                unit_window(3 * UNIT, starts, projected_f, low),
-                around(low, high),
+        def around(lanes):
+            rows = [slope_wide_f[first + i, pl.ds(second, 3), :, lanes] for i in range(3)]
+            return jnp.concatenate([r.reshape(3 * UNIT, 128) for r in rows], 0)
+
+        statistics = around(slice(D, D + 128))
+        for pairs in GROUPS:
+            results = pair_back(
+                [unit_window(3 * UNIT, starts, projected_f, pair * 128) for pair in pairs],
+                [around(lanes_of(pair)) for pair in pairs],
                 statistics,
-                keys,
-                values,
+                [with_columns(projected_f[middle, lanes_of(pair, D)], columns_ref[0, pair]) for pair in pairs],
+                [with_columns(projected_f[middle, lanes_of(pair, 2 * D)], columns_ref[1, pair]) for pair in pairs],
                 bias_back_ref[...],
             )
-            right_f[2, 0, own, low:high] = key_slope.astype(BF16)
-            right_f[3, 0, own, low:high] = value_slope.astype(BF16)
+            for pair, key_slope, value_slope in zip(pairs, *results):
+                right_f[2, 0, own, lanes_of(pair)] = key_slope.astype(BF16)
+                right_f[3, 0, own, lanes_of(pair)] = value_slope.astype(BF16)
 
     other = 3 - core
     twin_pair = start_twin(right_f.at[other, 0], right_f.at[other, 1])
@@ -759,6 +797,14 @@
     vmem = pl.BlockSpec(memory_space=pltpu.VMEM)
     hbm = pl.BlockSpec(memory_space=pl.ANY)
     select = merge_matrix()
+    constants = (
+        jnp.asarray(window_bias()),
+        jnp.asarray(window_bias_back()),
+        jnp.asarray(head_columns(), BF16),
+        jnp.asarray(statistic_columns(), BF16),
+        jnp.asarray(select, BF16),
+        jnp.asarray(select.T, BF16),
+    )
     per_batch = 2 * (lay.x - 1 + lay.y - 1) + lay.z - 1 + 2 * lay.y - 1
     copies = 5 * 8 + 7 + 3 * per_batch
     depth = lay.depth
@@ -774,7 +820,7 @@
             fine_shape,
             fine_shape,
         ),
-        in_specs=[vmem] * 10 + [hbm] * 5,
+        in_specs=[vmem] * 4 + [hbm] * 11,
         out_specs=[vmem] * 7,
         scratch_shapes=[
             pltpu.VMEM((D, 3 * D), BF16),
@@ -782,6 +828,7 @@
             pltpu.VMEM((4 * D, D), BF16),
             pltpu.VMEM((D, 3 * D), BF16),
             pltpu.VMEM((D, D), BF16),
+            *(pltpu.VMEM(c.shape, c.dtype) for c in constants),
             pltpu.VMEM((12, 16, D), F32),
             pltpu.VMEM((4 * UNIT, D), F32),
             pltpu.VMEM((4, 4, UNIT, D), BF16),
@@ -806,7 +853,7 @@
             *reducer_scratch(lay, lay.coarse_width),
             *reducer_scratch(lay, lay.fine_width),
             *reducer_scratch(lay, lay.fine_width),
-            pltpu.SemaphoreType.DMA((5,)),
+            pltpu.SemaphoreType.DMA((11,)),
             pltpu.SemaphoreType.DMA((copies,)),
             pltpu.SemaphoreType.DMA((copies,)),
         ],
@@ -818,17 +865,12 @@
         cotangent,
         fine_gain.reshape(1, D),
         coarse_gain.reshape(1, D),
-        jnp.asarray(window_bias()),
-        jnp.asarray(window_bias_back()),
-        jnp.asarray(head_columns(), BF16),
-        jnp.asarray(statistic_columns(), BF16),
-        jnp.asarray(select, BF16),
-        jnp.asarray(select.T, BF16),
         fine_attend,
         fine_output,
         merge_weight,
         coarse_attend,
         coarse_output,
+        *constants,
     )
     outs = pl.pallas_call(
         functools.partial(finish, lay),

time: 92 us -> 81.1 us (0.88)
  Pallas kernels: 91.1 us -> 80.3 us
    pallas_call x1, Pallas kernels: 89.2 us -> 78.4 us  [per_device(): pl.pallas_call(functools.partial(kernel, lay), out_shape=(jax.ShapeDtypeS...]
where the time goes in v3:
time: 81.1 us; the launch traced here: 81 us
  Pallas kernels  80.3 us (99%)
    pallas_call x1, Pallas kernels, per_device(): pl.pallas_call(functools.partial(kernel, lay), out_shape=(jax.ShapeDtypeS...  78.4 us
    pallas_call x1, Pallas kernels, per_device(): pl.pallas_call(functools.partial(finish, lay), out_shape=(jax.ShapeDtypeS...  1.9 us

profile of v3, /device:TPU:1, one launch (start us, length us, event | category | flops | bytes accessed | tf_op | source)
XLA Modules:
  0.0 81.0 jit_solution(7691810692943100884)
XLA Ops:
  0.6 78.4 %shard_map.214 = (bf16[1,6,6,512]{3,2,1,0:T(8,128)(2,1)}, bf16[1,12,12,512]{3,2,1,0:T(8,128)(2,1)}, f32[1,16]{1,0:T(1,128)}, f32[1,16]{1,0:T(1,128)}, bf16[2,4,1...) custom-call(bf16[1,12,12,512]{3,2,1,0:T(8,128)(2,1)} %tokens.1, ...), custom_call_target="tpu_custom_call" | custom-call | tf_op jit(solution)/shard_map/pallas_call | solution.py:812
  79.0 1.9 %shard_map.215 = (bf16[1,6,6,512]{3,2,1,0:T(8,128)(2,1)}, bf16[1,12,12,512]{3,2,1,0:T(8,128)(2,1)}, f32[1,16]{1,0:T(1,128)}, f32[16,1536]{1,0:T(8,128)}, f32[16,...) custom-call(bf16[1,6,6,512]{3,2,1,0:T(8,128)(2,1)} %get-tuple-element.25.refs_0, ...), custom_call_target="tpu_custom_call" | custom-call | tf_op jit(solution)/shard_map/pallas_call | solution.py:875

commit v4 on v3

--- a/solution.py
+++ b/solution.py
@@ -323,6 +323,57 @@
                 self.given[group, x, z, :, offset : offset + D] = shaped[block, run]
 
 
+class DeepReducer(Reducer):
+    def __init__(self, lay, place, wires, refs):
+        self.lay, self.place, self.wires = lay, place, wires
+        self.given, self.in_1, self.sum_2, self.in_2, self.sum_3, self.in_3, self.full = refs
+        self.copies = []
+
+    def first_start(self):
+        lay, here = self.lay, self.place
+        for step in range(1, lay.z):
+            z = (here["z"] + step) % lay.z
+            self.send(self.given.at[:, :, z], self.in_1.at[step - 1], self.device(z=z))
+
+    def first_finish(self):
+        self.arrive()
+        lay, here = self.lay, self.place
+
+        @pl.loop(0, lay.y)
+        def _(y):
+            total = self.given[y, :, here["z"]].astype(F32)
+            for k in range(lay.z - 1):
+                total += self.in_1[k, y].astype(F32)
+            self.sum_2[y] = total.astype(BF16)
+
+    def second_start(self):
+        lay, here = self.lay, self.place
+        for step in range(1, lay.x):
+            x = (here["x"] + step) % lay.x
+            self.send(self.sum_2.at[:, x], self.in_2.at[step - 1], self.device(x=x))
+
+    def second_finish(self):
+        self.arrive()
+        total = self.sum_2[:, self.place["x"]].astype(F32)
+        for k in range(self.lay.x - 1):
+            total += self.in_2[k].astype(F32)
+        self.sum_3[...] = total.astype(BF16)
+
+    def third_start(self):
+        lay, here = self.lay, self.place
+        for step in range(1, lay.y):
+            y = (here["y"] + step) % lay.y
+            self.send(self.sum_3.at[y], self.in_3.at[step - 1], self.device(y=y))
+
+    def third_finish(self):
+        self.arrive()
+        here = self.place
+        total = self.sum_3[here["y"]].astype(F32)
+        for k in range(self.lay.y - 1):
+            total += self.in_3[k].astype(F32)
+        self.full[here["core"], here["y"]] = total.astype(BF16)
+
+
 GROUPS = ((0, 1, 2, 3),)
 
 
@@ -357,7 +408,7 @@
     field_c, wide_c, slope_wide_c, projected_c, mixed_slope_c, attention_c, exact_c, lse_c, statistics_c, factors_c,
     *rest,
 ):
-    load_sem, send_sem, recv_sem = rest[30:]
+    load_sem, send_sem, recv_sem = rest[27:]
     sec, lat, lon = (lax.axis_index(k) for k in ("sec", "lat", "lon"))
     core = lat % 2
     place = {"core": core, "y": lat // 2 * lay.sec + sec, "x": lon // lay.z, "z": lon % lay.z}
@@ -407,8 +458,8 @@
         return copy
 
     coarse_sum = Reducer(lay, place, wires, rest[:10])
-    early_sum = Reducer(lay, place, wires, rest[10:20])
-    late_sum = Reducer(lay, place, wires, rest[20:30])
+    early_sum = DeepReducer(lay, place, wires, rest[10:17])
+    late_sum = Reducer(lay, place, wires, rest[17:27])
 
     barrier = pltpu.get_barrier_semaphore()
     peers = [neighbour(step) for step in AROUND]
@@ -639,26 +690,6 @@
     rims = fine_rims(slope_wide_f)
     twin_slope = start_twin(right_f.at[1, 0], right_f.at[1, 1])
 
-    twin_factors.wait()
-    twin_merged.wait()
-
-    def both(index):
-        return factors_c[index].reshape(2 * UNIT, D)
-
-    @pl.when(core == 0)
-    def _():
-        for k in range(3):
-            coarse_sum.put(k * D, t_dot(both(0), both(1 + k)))
-        coarse_sum.put(3 * D, t_dot(both(4), both(5)))
-
-    @pl.when(core == 1)
-    def _():
-        for k in range(4):
-            rows = slice(k * UNIT, (k + 1) * UNIT)
-            coarse_sum.put_merged(k, t_dot(merged[:, rows].reshape(2 * UNIT, D), both(6)))
-
-    coarse_sum.first_start()
-
     @pl.loop(0, 4)
     def _(quad):
         own, starts = own_of(quad), starts_of(quad)
@@ -673,6 +704,25 @@
                 right_f[0, 0, own, lanes_of(pair)] = query_slope.astype(BF16)
 
     twin_query = start_twin(right_f.at[0, 0], right_f.at[0, 1])
+    twin_factors.wait()
+    twin_merged.wait()
+
+    def both(index):
+        return factors_c[index].reshape(2 * UNIT, D)
+
+    @pl.when(core == 0)
+    def _():
+        for k in range(3):
+            coarse_sum.put(k * D, t_dot(both(0), both(1 + k)))
+        coarse_sum.put(3 * D, t_dot(both(4), both(5)))
+
+    @pl.when(core == 1)
+    def _():
+        for k in range(4):
+            rows = slice(k * UNIT, (k + 1) * UNIT)
+            coarse_sum.put_merged(k, t_dot(merged[:, rows].reshape(2 * UNIT, D), both(6)))
+
+    coarse_sum.first_start()
     twin_hidden.wait()
     twin_mixed.wait()
     twin_slope.wait()
@@ -782,6 +832,13 @@
     return [pltpu.VMEM(shape + end, BF16) for shape in shapes]
 
 
+def deep_scratch(lay, width):
+    y, x, z = lay.y, lay.x, lay.z
+    end = (lay.depth, width)
+    shapes = ((y, x, z), (z - 1, y, x), (y, x), (x - 1, y), (y,), (y - 1,), (2, y))
+    return [pltpu.VMEM(shape + end, BF16) for shape in shapes]
+
+
 def per_device(
     lay,
     tokens,
@@ -806,7 +863,8 @@
         jnp.asarray(select.T, BF16),
     )
     per_batch = 2 * (lay.x - 1 + lay.y - 1) + lay.z - 1 + 2 * lay.y - 1
-    copies = 5 * 8 + 7 + 3 * per_batch
+    deep_batch = lay.z - 1 + lay.x - 1 + lay.y - 1 + 2 * lay.y - 1
+    copies = 5 * 8 + 7 + 2 * per_batch + deep_batch
     depth = lay.depth
     fine_shape = jax.ShapeDtypeStruct((2, lay.y, depth, lay.fine_width), BF16)
     between = pl.pallas_call(
@@ -851,7 +909,7 @@
             pltpu.VMEM((3, 3, UNIT, 128), BF16),
             pltpu.VMEM((7, 2, UNIT, D), BF16),
             *reducer_scratch(lay, lay.coarse_width),
-            *reducer_scratch(lay, lay.fine_width),
+            *deep_scratch(lay, lay.fine_width),
             *reducer_scratch(lay, lay.fine_width),
             pltpu.SemaphoreType.DMA((11,)),
             pltpu.SemaphoreType.DMA((copies,)),

time: 81.1 us -> 82 us (1.011)
    pallas_call x1, Pallas kernels: 78.4 us -> 79.2 us  [per_device(): pl.pallas_call(functools.partial(kernel, lay), out_shape=(jax.ShapeDtypeS...]
where the time goes in v4:
time: 82 us; the launch traced here: 81.9 us
  Pallas kernels  81.1 us (99%)
    pallas_call x1, Pallas kernels, per_device(): pl.pallas_call(functools.partial(kernel, lay), out_shape=(jax.ShapeDtypeS...  79.2 us
    pallas_call x1, Pallas kernels, per_device(): pl.pallas_call(functools.partial(finish, lay), out_shape=(jax.ShapeDtypeS...  1.9 us

profile of v4, /device:TPU:1, one launch (start us, length us, event | category | flops | bytes accessed | tf_op | source)
XLA Modules:
  0.0 81.9 jit_solution(17528785709015636158)
XLA Ops:
  0.6 79.2 %shard_map.214 = (bf16[1,6,6,512]{3,2,1,0:T(8,128)(2,1)}, bf16[1,12,12,512]{3,2,1,0:T(8,128)(2,1)}, f32[1,16]{1,0:T(1,128)}, f32[1,16]{1,0:T(1,128)}, bf16[2,4,1...) custom-call(bf16[1,12,12,512]{3,2,1,0:T(8,128)(2,1)} %tokens.1, ...), custom_call_target="tpu_custom_call" | custom-call | tf_op jit(solution)/shard_map/pallas_call | solution.py:870
  79.9 1.9 %shard_map.215 = (bf16[1,6,6,512]{3,2,1,0:T(8,128)(2,1)}, bf16[1,12,12,512]{3,2,1,0:T(8,128)(2,1)}, f32[1,16]{1,0:T(1,128)}, f32[16,1536]{1,0:T(8,128)}, f32[16,...) custom-call(bf16[1,6,6,512]{3,2,1,0:T(8,128)(2,1)} %get-tuple-element.25.refs_0, ...), custom_call_target="tpu_custom_call" | custom-call | tf_op jit(solution)/shard_map/pallas_call | solution.py:933

commit v5 on v4

--- a/solution.py
+++ b/solution.py
@@ -278,8 +278,11 @@
         self.full[here["core"], here["y"]] = total.astype(BF16)
 
     def last_start(self):
+        self.spread(self.full)
+
+    def spread(self, ref):
         lay, here = self.lay, self.place
-        own = self.full.at[here["core"], here["y"]]
+        own = ref.at[here["core"], here["y"]]
         for across in range(2):
             for step in range(lay.y):
                 if across or step:
@@ -326,7 +329,7 @@
 class DeepReducer(Reducer):
     def __init__(self, lay, place, wires, refs):
         self.lay, self.place, self.wires = lay, place, wires
-        self.given, self.in_1, self.sum_2, self.in_2, self.sum_3, self.in_3, self.full = refs
+        self.given, self.in_1, self.sum_2, self.in_2, self.parts, self.full = refs
         self.copies = []
 
     def first_start(self):
@@ -354,24 +357,24 @@
 
     def second_finish(self):
         self.arrive()
-        total = self.sum_2[:, self.place["x"]].astype(F32)
+        here = self.place
+        total = self.sum_2[:, here["x"]].astype(F32)
         for k in range(self.lay.x - 1):
             total += self.in_2[k].astype(F32)
-        self.sum_3[...] = total.astype(BF16)
-
-    def third_start(self):
-        lay, here = self.lay, self.place
-        for step in range(1, lay.y):
-            y = (here["y"] + step) % lay.y
-            self.send(self.sum_3.at[y], self.in_3.at[step - 1], self.device(y=y))
-
-    def third_finish(self):
+        self.parts[here["core"], here["y"]] = total.astype(BF16)
+
+    def last_start(self):
+        self.spread(self.parts)
+
+    def last_finish(self):
         self.arrive()
-        here = self.place
-        total = self.sum_3[here["y"]].astype(F32)
-        for k in range(self.lay.y - 1):
-            total += self.in_3[k].astype(F32)
-        self.full[here["core"], here["y"]] = total.astype(BF16)
+
+        @pl.loop(0, 2)
+        def _(core):
+            total = self.parts[core, 0].astype(F32)
+            for y in range(1, self.lay.y):
+                total += self.parts[core, y].astype(F32)
+            self.full[core] = total.astype(BF16)
 
 
 GROUPS = ((0, 1, 2, 3),)
@@ -398,17 +401,18 @@
 
 def kernel(
     lay,
-    tokens, cotangent, fine_gain, coarse_gain,
+    tokens_hbm, cotangent_hbm, fine_gain, coarse_gain,
     fine_attend_hbm, fine_output_hbm, merge_hbm, coarse_attend_hbm, coarse_output_hbm,
     bias_hbm, bias_back_hbm, heads_hbm, columns_hbm, merge_ref_hbm, split_hbm,
-    coarse_field, token_gradient, fine_gain_out, coarse_gain_out, coarse_full, early_full, late_full,
+    coarse_field_hbm, token_gradient_hbm, fine_gain_out, coarse_gain_out, coarse_full, early_full, late_full,
+    tokens, cotangent, coarse_field, token_gradient,
     fine_attend, fine_output, merge_weight, coarse_attend, coarse_output,
     bias_ref, bias_back_ref, heads_ref, columns_ref, merge_ref, split_ref,
     strip, field_f, wide_f, projected_f, attention_f, exact_f, lse_f, slope_wide_f, left_f, right_f, merged,
     field_c, wide_c, slope_wide_c, projected_c, mixed_slope_c, attention_c, exact_c, lse_c, statistics_c, factors_c,
     *rest,
 ):
-    load_sem, send_sem, recv_sem = rest[27:]
+    load_sem, send_sem, recv_sem = rest[26:]
     sec, lat, lon = (lax.axis_index(k) for k in ("sec", "lat", "lon"))
     core = lat % 2
     place = {"core": core, "y": lat // 2 * lay.sec + sec, "x": lon // lay.z, "z": lon % lay.z}
@@ -458,8 +462,8 @@
         return copy
 
     coarse_sum = Reducer(lay, place, wires, rest[:10])
-    early_sum = DeepReducer(lay, place, wires, rest[10:17])
-    late_sum = Reducer(lay, place, wires, rest[17:27])
+    early_sum = DeepReducer(lay, place, wires, rest[10:16])
+    late_sum = Reducer(lay, place, wires, rest[16:26])
 
     barrier = pltpu.get_barrier_semaphore()
     peers = [neighbour(step) for step in AROUND]
@@ -478,6 +482,8 @@
         name: pltpu.make_async_copy(source, target, load_sem.at[i])
         for i, (name, source, target) in enumerate(
             (
+                ("tokens", tokens_hbm, tokens),
+                ("cotangent", cotangent_hbm, cotangent),
                 ("fine_attend", fine_attend_hbm, fine_attend),
                 ("bias_ref", bias_hbm, bias_ref),
                 ("fine_output", fine_output_hbm, fine_output),
@@ -497,6 +503,7 @@
 
     field_f[...] = jnp.zeros_like(field_f)
     field_c[...] = jnp.zeros_like(field_c)
+    loads["tokens"].wait()
     for row in range(12):
         strip[row, :12] = tokens[0, row].astype(F32)
     for row in range(12):
@@ -505,6 +512,7 @@
             field_f[start : start + 6] = strip[row, 6 * half : 6 * half + 6]
     for unit in range(4):
         wide_f[1 + unit // 2, 1 + unit % 2] = field_f[unit * UNIT : (unit + 1) * UNIT].astype(BF16)
+    loads["cotangent"].wait()
     for row in range(6):
         field_c[row * 8 : row * 8 + 6] = cotangent[0, row].astype(F32)
     slope_wide_c[1, 1] = field_c[...].astype(BF16)
@@ -582,7 +590,7 @@
     def own_of(quad):
         return pl.ds(pl.multiple_of(quad * UNIT, UNIT), UNIT)
 
-    @pl.loop(0, 4)
+    @pl.loop(0, 4, unroll=4)
     def _(quad):
         first = quad // 2
         own, middle, starts = own_of(quad), middle_of(quad), starts_of(quad)
@@ -645,6 +653,8 @@
     moved = field_c[...] + dot(factors_c[4, 0], coarse_output[...])
     for row in range(6):
         coarse_field[0, row] = moved[row * 8 : row * 8 + 6].astype(BF16)
+    field_store = pltpu.make_async_copy(coarse_field, coarse_field_hbm, load_sem.at[13])
+    field_store.start()
     for pairs in GROUPS:
         results = query_back(
             [projected_c[:, lanes_of(pair, D)] for pair in pairs],
@@ -690,7 +700,7 @@
     rims = fine_rims(slope_wide_f)
     twin_slope = start_twin(right_f.at[1, 0], right_f.at[1, 1])
 
-    @pl.loop(0, 4)
+    @pl.loop(0, 4, unroll=4)
     def _(quad):
         own, starts = own_of(quad), starts_of(quad)
         for pairs in GROUPS:
@@ -731,7 +741,7 @@
     wait_rims(rims)
     early_sum.first_start()
 
-    @pl.loop(0, 4)
+    @pl.loop(0, 4, unroll=4)
     def _(quad):
         own, middle, starts = own_of(quad), middle_of(quad), starts_of(quad)
         first, second = quad // 2, quad % 2
@@ -764,8 +774,6 @@
     late_sum.first_start()
     coarse_sum.first_finish()
     coarse_sum.second_start()
-    early_sum.first_finish()
-    early_sum.second_start()
     slope = input_back(right_f[1, 0].astype(F32), hidden_slope, field_f[...], gain_f)
     for row in range(12):
         for half in range(2):
@@ -773,17 +781,19 @@
             strip[row, 6 * half : 6 * half + 6] = slope[start : start + 6]
     for row in range(12):
         token_gradient[0, row] = strip[row, :12].astype(BF16)
+    gradient_store = pltpu.make_async_copy(token_gradient, token_gradient_hbm, load_sem.at[14])
+    gradient_store.start()
     late_sum.first_finish()
     late_sum.second_start()
     coarse_sum.second_finish()
     coarse_sum.third_start()
-    early_sum.second_finish()
-    early_sum.third_start()
+    early_sum.first_finish()
+    early_sum.second_start()
     late_sum.second_finish()
     late_sum.third_start()
     coarse_sum.third_finish()
     coarse_sum.last_start()
-    early_sum.third_finish()
+    early_sum.second_finish()
     early_sum.last_start()
     late_sum.third_finish()
     late_sum.last_start()
@@ -794,6 +804,8 @@
     early_full[...] = early_sum.full[...]
     late_sum.last_finish()
     late_full[...] = late_sum.full[...]
+    field_store.wait()
+    gradient_store.wait()
     total = jnp.concatenate([early_sum.column(0, D), late_sum.column(0, 2 * D)], 1)
     fine_gain_out[...] = gain_back(lay, lon, total, fine_attend, gain_f)
 
@@ -835,7 +847,7 @@
 def deep_scratch(lay, width):
     y, x, z = lay.y, lay.x, lay.z
     end = (lay.depth, width)
-    shapes = ((y, x, z), (z - 1, y, x), (y, x), (x - 1, y), (y,), (y - 1,), (2, y))
+    shapes = ((y, x, z), (z - 1, y, x), (y, x), (x - 1, y), (2, y, y), (2, y))
     return [pltpu.VMEM(shape + end, BF16) for shape in shapes]
 
 
@@ -863,7 +875,7 @@
         jnp.asarray(select.T, BF16),
     )
     per_batch = 2 * (lay.x - 1 + lay.y - 1) + lay.z - 1 + 2 * lay.y - 1
-    deep_batch = lay.z - 1 + lay.x - 1 + lay.y - 1 + 2 * lay.y - 1
+    deep_batch = lay.z - 1 + lay.x - 1 + 2 * lay.y - 1
     copies = 5 * 8 + 7 + 2 * per_batch + deep_batch
     depth = lay.depth
     fine_shape = jax.ShapeDtypeStruct((2, lay.y, depth, lay.fine_width), BF16)
@@ -878,9 +890,13 @@
             fine_shape,
             fine_shape,
         ),
-        in_specs=[vmem] * 4 + [hbm] * 11,
-        out_specs=[vmem] * 7,
+        in_specs=[hbm] * 2 + [vmem] * 2 + [hbm] * 11,
+        out_specs=[hbm] * 2 + [vmem] * 5,
         scratch_shapes=[
+            pltpu.VMEM(tokens.shape, BF16),
+            pltpu.VMEM(cotangent.shape, BF16),
+            pltpu.VMEM(cotangent.shape, BF16),
+            pltpu.VMEM(tokens.shape, BF16),
             pltpu.VMEM((D, 3 * D), BF16),
             pltpu.VMEM((D, D), BF16),
             pltpu.VMEM((4 * D, D), BF16),
@@ -911,7 +927,7 @@
             *reducer_scratch(lay, lay.coarse_width),
             *deep_scratch(lay, lay.fine_width),
             *reducer_scratch(lay, lay.fine_width),
-            pltpu.SemaphoreType.DMA((11,)),
+            pltpu.SemaphoreType.DMA((15,)),
             pltpu.SemaphoreType.DMA((copies,)),
             pltpu.SemaphoreType.DMA((copies,)),
         ],

time: 82 us -> 79 us (0.963)
  Pallas kernels: 81.1 us -> 78.1 us
    pallas_call x1, Pallas kernels: 79.2 us -> 76.2 us  [per_device(): pl.pallas_call(functools.partial(kernel, lay), out_shape=(jax.ShapeDtypeS...]
where the time goes in v5:
time: 79 us; the launch traced here: 78.9 us
  Pallas kernels  78.1 us (99%)
    pallas_call x1, Pallas kernels, per_device(): pl.pallas_call(functools.partial(kernel, lay), out_shape=(jax.ShapeDtypeS...  76.2 us
    pallas_call x1, Pallas kernels, per_device(): pl.pallas_call(functools.partial(finish, lay), out_shape=(jax.ShapeDtypeS...  1.9 us

profile of v5, /device:TPU:1, one launch (start us, length us, event | category | flops | bytes accessed | tf_op | source)
XLA Modules:
  0.0 78.9 jit_solution(13295930474808139278)
XLA Ops:
  0.6 76.2 %shard_map.214 = (bf16[1,6,6,512]{3,2,1,0:T(8,128)(2,1)}, bf16[1,12,12,512]{3,2,1,0:T(8,128)(2,1)}, f32[1,16]{1,0:T(1,128)}, f32[1,16]{1,0:T(1,128)}, bf16[2,4,1...) custom-call(bf16[1,12,12,512]{3,2,1,0:T(8,128)(2,1)} %tokens_hbm.1, ...), custom_call_target="tpu_custom_call" | custom-call | tf_op jit(solution)/shard_map/pallas_call | solution.py:882
  76.9 1.9 %shard_map.215 = (bf16[1,6,6,512]{3,2,1,0:T(8,128)(2,1)}, bf16[1,12,12,512]{3,2,1,0:T(8,128)(2,1)}, f32[1,16]{1,0:T(1,128)}, f32[16,1536]{1,0:T(8,128)}, f32[16,...) custom-call(bf16[1,6,6,512]{3,2,1,0:T(8,128)(2,1)} %get-tuple-element.25.refs_0, ...), custom_call_target="tpu_custom_call" | custom-call | tf_op jit(solution)/shard_map/pallas_call | solution.py:949

commit v6 on v5

--- a/solution.py
+++ b/solution.py
@@ -185,8 +185,8 @@
 
 
 class Reducer:
-    def __init__(self, lay, place, wires, refs):
-        self.lay, self.place, self.wires = lay, place, wires
+    def __init__(self, lay, place, wires, pending, refs):
+        self.lay, self.place, self.wires, self.pending = lay, place, wires, pending
         (
             self.given, self.in_1a, self.in_1b, self.sum_2a, self.sum_2b,
             self.in_2a, self.in_2b, self.sum_3, self.in_3, self.full,
@@ -205,10 +205,11 @@
         copy = self.wires(source, target, device)
         copy.start()
         self.copies.append(copy)
+        self.pending.append((copy, None))
 
     def arrive(self):
         for copy in self.copies:
-            copy.wait()
+            copy.wait_recv()
         self.copies = []
 
     def first_start(self):
@@ -327,8 +328,8 @@
 
 
 class DeepReducer(Reducer):
-    def __init__(self, lay, place, wires, refs):
-        self.lay, self.place, self.wires = lay, place, wires
+    def __init__(self, lay, place, wires, pending, refs):
+        self.lay, self.place, self.wires, self.pending = lay, place, wires, pending
         self.given, self.in_1, self.sum_2, self.in_2, self.parts, self.full = refs
         self.copies = []
 
@@ -388,9 +389,13 @@
     return jnp.concatenate([stack_heads(part), columns], 1)
 
 
-def gain_back(lay, lon, total, weight, gain):
-    own = weight[pl.ds(pl.multiple_of(lon * lay.depth, lay.depth), lay.depth), :].astype(F32)
-    column = jnp.sum(total * own, axis=1, keepdims=True)
+def gain_column(lay, lon, total, weight, start):
+    rows = pl.ds(pl.multiple_of(lon * lay.depth, lay.depth), lay.depth)
+    own = weight[rows, start : start + total.shape[1]].astype(F32)
+    return jnp.sum(total * own, axis=1, keepdims=True)
+
+
+def gain_back(lay, lon, column, gain):
     row = lax.broadcasted_iota(jnp.int32, (lay.depth, D), 0) + lon * lay.depth
     at = lax.broadcasted_iota(jnp.int32, (lay.depth, D), 1) == row
     column = column / jnp.sum(jnp.where(at, gain, 0.0), axis=1, keepdims=True)
@@ -417,6 +422,7 @@
     core = lat % 2
     place = {"core": core, "y": lat // 2 * lay.sec + sec, "x": lon // lay.z, "z": lon % lay.z}
     used = [0]
+    pending = []
 
     def wires(source, target, device):
         index = used[0]
@@ -442,28 +448,30 @@
                 sends = lat != (last if step[0] > 0 else 0)
                 takes = lat != (0 if step[0] > 0 else last)
                 pl.when(sends)(copy.start)
-                copies.append((copy, sends, takes))
+                copies.append((copy, takes))
+                pending.append((copy, sends))
             else:
                 copy.start()
-                copies.append((copy, None, None))
+                copies.append((copy, None))
+                pending.append((copy, None))
         return copies
 
     def wait_rims(copies):
-        for copy, sends, takes in copies:
-            if sends is None:
-                copy.wait()
+        for copy, takes in copies:
+            if takes is None:
+                copy.wait_recv()
             else:
-                pl.when(sends)(copy.wait_send)
                 pl.when(takes)(copy.wait_recv)
 
     def start_twin(source, target):
         copy = wires(source, target, coarse_sum.device(core=1 - core))
         copy.start()
+        pending.append((copy, None))
         return copy
 
-    coarse_sum = Reducer(lay, place, wires, rest[:10])
-    early_sum = DeepReducer(lay, place, wires, rest[10:16])
-    late_sum = Reducer(lay, place, wires, rest[16:26])
+    coarse_sum = Reducer(lay, place, wires, pending, rest[:10])
+    early_sum = DeepReducer(lay, place, wires, pending, rest[10:16])
+    late_sum = Reducer(lay, place, wires, pending, rest[16:26])
 
     barrier = pltpu.get_barrier_semaphore()
     peers = [neighbour(step) for step in AROUND]
@@ -714,8 +722,8 @@
                 right_f[0, 0, own, lanes_of(pair)] = query_slope.astype(BF16)
 
     twin_query = start_twin(right_f.at[0, 0], right_f.at[0, 1])
-    twin_factors.wait()
-    twin_merged.wait()
+    twin_factors.wait_recv()
+    twin_merged.wait_recv()
 
     def both(index):
         return factors_c[index].reshape(2 * UNIT, D)
@@ -733,10 +741,10 @@
             coarse_sum.put_merged(k, t_dot(merged[:, rows].reshape(2 * UNIT, D), both(6)))
 
     coarse_sum.first_start()
-    twin_hidden.wait()
-    twin_mixed.wait()
-    twin_slope.wait()
-    twin_query.wait()
+    twin_hidden.wait_recv()
+    twin_mixed.wait_recv()
+    twin_slope.wait_recv()
+    twin_query.wait_recv()
     early_sum.put(0, t_dot(left_f[core].reshape(8 * UNIT, D), right_f[core].reshape(8 * UNIT, D)))
     wait_rims(rims)
     early_sum.first_start()
@@ -769,7 +777,7 @@
     hidden_slope = dot_t(right_f[0, 0], fine_attend[:, :D])
     hidden_slope += dot_t(right_f[2, 0], fine_attend[:, D : 2 * D])
     hidden_slope += dot_t(right_f[3, 0], fine_attend[:, 2 * D :])
-    twin_pair.wait()
+    twin_pair.wait_recv()
     late_sum.put(0, t_dot(left_f[0].reshape(8 * UNIT, D), right_f[2 + core].reshape(8 * UNIT, D)))
     late_sum.first_start()
     coarse_sum.first_finish()
@@ -799,15 +807,22 @@
     late_sum.last_start()
     coarse_sum.last_finish()
     coarse_full[...] = coarse_sum.full[...]
-    coarse_gain_out[...] = gain_back(lay, lon, coarse_sum.column(0, 3 * D), coarse_attend, gain_c)
+    column = gain_column(lay, lon, coarse_sum.column(0, 3 * D), coarse_attend, 0)
+    coarse_gain_out[...] = gain_back(lay, lon, column, gain_c)
     early_sum.last_finish()
     early_full[...] = early_sum.full[...]
+    column = gain_column(lay, lon, early_sum.column(0, D), fine_attend, 0)
+    field_store.wait()
+    gradient_store.wait()
+    for copy, sends in pending:
+        if sends is None:
+            copy.wait_send()
+        else:
+            pl.when(sends)(copy.wait_send)
     late_sum.last_finish()
     late_full[...] = late_sum.full[...]
-    field_store.wait()
-    gradient_store.wait()
-    total = jnp.concatenate([early_sum.column(0, D), late_sum.column(0, 2 * D)], 1)
-    fine_gain_out[...] = gain_back(lay, lon, total, fine_attend, gain_f)
+    column += gain_column(lay, lon, late_sum.column(0, 2 * D), fine_attend, D)
+    fine_gain_out[...] = gain_back(lay, lon, column, gain_f)
 
 
 def finish(lay, *refs):
@@ -822,7 +837,7 @@
     coarse_gain_out[...] = coarse_gain[...]
 
     def column(full, start, width):
-        return Reducer(lay, None, None, (None,) * 9 + (full,)).column(start, width)
+        return Reducer(lay, None, None, None, (None,) * 9 + (full,)).column(start, width)
 
     for k in range(3):
         fine_attend[:, k * D : (k + 1) * D] = column(late_full, (k - 1) * D, D) if k else column(early_full, 0, D)

time: 79 us -> 79 us (level)
  no operation moved by 1% of the time
where the time goes in v6:
time: 79 us; the launch traced here: 78.9 us
  Pallas kernels  78.1 us (99%)
    pallas_call x1, Pallas kernels, per_device(): pl.pallas_call(functools.partial(kernel, lay), out_shape=(jax.ShapeDtypeS...  76.2 us
    pallas_call x1, Pallas kernels, per_device(): pl.pallas_call(functools.partial(finish, lay), out_shape=(jax.ShapeDtypeS...  1.9 us

profile of v6, /device:TPU:1, one launch (start us, length us, event | category | flops | bytes accessed | tf_op | source)
XLA Modules:
  0.0 78.9 jit_solution(6381913426016349900)
XLA Ops:
  0.6 76.2 %shard_map.214 = (bf16[1,6,6,512]{3,2,1,0:T(8,128)(2,1)}, bf16[1,12,12,512]{3,2,1,0:T(8,128)(2,1)}, f32[1,16]{1,0:T(1,128)}, f32[1,16]{1,0:T(1,128)}, bf16[2,4,1...) custom-call(bf16[1,12,12,512]{3,2,1,0:T(8,128)(2,1)} %tokens_hbm.1, ...), custom_call_target="tpu_custom_call" | custom-call | tf_op jit(solution)/shard_map/pallas_call | solution.py:897
  76.9 1.9 %shard_map.215 = (bf16[1,6,6,512]{3,2,1,0:T(8,128)(2,1)}, bf16[1,12,12,512]{3,2,1,0:T(8,128)(2,1)}, f32[1,16]{1,0:T(1,128)}, f32[16,1536]{1,0:T(8,128)}, f32[16,...) custom-call(bf16[1,6,6,512]{3,2,1,0:T(8,128)(2,1)} %get-tuple-element.25.refs_0, ...), custom_call_target="tpu_custom_call" | custom-call | tf_op jit(solution)/shard_map/pallas_call | solution.py:964

commit v7 on v6

--- a/solution.py
+++ b/solution.py
@@ -18,7 +18,7 @@
 MESH = pl.DeviceIdType.MESH
 F32 = jnp.float32
 BF16 = jnp.bfloat16
-AROUND = ((0, 1), (0, -1), (1, 0), (-1, 0), (1, 1), (1, -1), (-1, 1), (-1, -1))
+AROUND = ((1, 1), (1, -1), (-1, 1), (-1, -1), (0, 1), (0, -1), (1, 0), (-1, 0))
 
 
 def dot(left, right):
@@ -184,6 +184,10 @@
     return slope + factor * (scaled - normed * jnp.mean(scaled * normed, axis=-1, keepdims=True))
 
 
+def far_first(size):
+    return sorted(range(1, size), key=lambda step: -min(step, size - step))
+
+
 class Reducer:
     def __init__(self, lay, place, wires, pending, refs):
         self.lay, self.place, self.wires, self.pending = lay, place, wires, pending
@@ -216,10 +220,10 @@
         lay, here = self.lay, self.place
         low = pl.ds(0, lay.z_low)
         high = pl.ds(lay.z_low, lay.z - lay.z_low)
-        for step in range(1, lay.x):
+        for step in far_first(lay.x):
             x = (here["x"] + step) % lay.x
             self.send(self.given.at[:, x, low], self.in_1a.at[step - 1], self.device(x=x))
-        for step in range(1, lay.y):
+        for step in far_first(lay.y):
             y = (here["y"] + step) % lay.y
             self.send(self.given.at[y, :, high], self.in_1b.at[step - 1], self.device(y=y))
 
@@ -245,10 +249,10 @@
 
     def second_start(self):
         lay, here = self.lay, self.place
-        for step in range(1, lay.y):
+        for step in far_first(lay.y):
             y = (here["y"] + step) % lay.y
             self.send(self.sum_2a.at[y], self.in_2a.at[step - 1], self.device(y=y))
-        for step in range(1, lay.x):
+        for step in far_first(lay.x):
             x = (here["x"] + step) % lay.x
             self.send(self.sum_2b.at[x], self.in_2b.at[step - 1], self.device(x=x))
 
@@ -266,7 +270,7 @@
 
     def third_start(self):
         lay, here = self.lay, self.place
-        for step in range(1, lay.z):
+        for step in far_first(lay.z):
             z = (here["z"] + step) % lay.z
             self.send(self.sum_3.at[z], self.in_3.at[step - 1], self.device(z=z))
 
@@ -279,19 +283,22 @@
         self.full[here["core"], here["y"]] = total.astype(BF16)
 
     def last_start(self):
-        self.spread(self.full)
-
-    def spread(self, ref):
-        lay, here = self.lay, self.place
-        own = ref.at[here["core"], here["y"]]
-        for across in range(2):
-            for step in range(lay.y):
-                if across or step:
-                    core = (here["core"] + across) % 2
-                    y = (here["y"] + step) % lay.y
-                    self.send(own, own, self.device(core=core, y=y))
+        here = self.place
+        self.spread(self.full.at[here["core"], here["y"]])
+
+    def spread(self, own):
+        for step in far_first(self.lay.y):
+            self.send(own, own, self.device(y=(self.place["y"] + step) % self.lay.y))
 
     def last_finish(self):
+        self.arrive()
+
+    def share_start(self):
+        core = self.place["core"]
+        half = self.full.at[core]
+        self.send(half, half, self.device(core=1 - core))
+
+    def share_finish(self):
         self.arrive()
 
     def column(self, start, width):
@@ -335,7 +342,7 @@
 
     def first_start(self):
         lay, here = self.lay, self.place
-        for step in range(1, lay.z):
+        for step in far_first(lay.z):
             z = (here["z"] + step) % lay.z
             self.send(self.given.at[:, :, z], self.in_1.at[step - 1], self.device(z=z))
 
@@ -352,7 +359,7 @@
 
     def second_start(self):
         lay, here = self.lay, self.place
-        for step in range(1, lay.x):
+        for step in far_first(lay.x):
             x = (here["x"] + step) % lay.x
             self.send(self.sum_2.at[:, x], self.in_2.at[step - 1], self.device(x=x))
 
@@ -362,20 +369,17 @@
         total = self.sum_2[:, here["x"]].astype(F32)
         for k in range(self.lay.x - 1):
             total += self.in_2[k].astype(F32)
-        self.parts[here["core"], here["y"]] = total.astype(BF16)
+        self.parts[here["y"]] = total.astype(BF16)
 
     def last_start(self):
-        self.spread(self.parts)
+        self.spread(self.parts.at[self.place["y"]])
 
     def last_finish(self):
         self.arrive()
-
-        @pl.loop(0, 2)
-        def _(core):
-            total = self.parts[core, 0].astype(F32)
-            for y in range(1, self.lay.y):
-                total += self.parts[core, y].astype(F32)
-            self.full[core] = total.astype(BF16)
+        total = self.parts[0].astype(F32)
+        for y in range(1, self.lay.y):
+            total += self.parts[y].astype(F32)
+        self.full[self.place["core"]] = total.astype(BF16)
 
 
 GROUPS = ((0, 1, 2, 3),)
@@ -477,12 +481,8 @@
     peers = [neighbour(step) for step in AROUND]
     peers += [coarse_sum.device(x=(place["x"] + s) % lay.x) for s in range(1, lay.x)]
     peers += [coarse_sum.device(z=(place["z"] + s) % lay.z) for s in range(1, lay.z)]
-    peers += [
-        coarse_sum.device(core=(core + c) % 2, y=(place["y"] + s) % lay.y)
-        for c in range(2)
-        for s in range(lay.y)
-        if c or s
-    ]
+    peers += [coarse_sum.device(y=(place["y"] + s) % lay.y) for s in range(1, lay.y)]
+    peers += [coarse_sum.device(core=1 - core)]
     for peer in peers:
         pl.semaphore_signal(barrier, inc=1, device_id=peer, device_id_type=MESH)
 
@@ -806,10 +806,16 @@
     late_sum.third_finish()
     late_sum.last_start()
     coarse_sum.last_finish()
+    coarse_sum.share_start()
+    early_sum.last_finish()
+    early_sum.share_start()
+    late_sum.last_finish()
+    late_sum.share_start()
+    coarse_sum.share_finish()
     coarse_full[...] = coarse_sum.full[...]
     column = gain_column(lay, lon, coarse_sum.column(0, 3 * D), coarse_attend, 0)
     coarse_gain_out[...] = gain_back(lay, lon, column, gain_c)
-    early_sum.last_finish()
+    early_sum.share_finish()
     early_full[...] = early_sum.full[...]
     column = gain_column(lay, lon, early_sum.column(0, D), fine_attend, 0)
     field_store.wait()
@@ -819,7 +825,7 @@
             copy.wait_send()
         else:
             pl.when(sends)(copy.wait_send)
-    late_sum.last_finish()
+    late_sum.share_finish()
     late_full[...] = late_sum.full[...]
     column += gain_column(lay, lon, late_sum.column(0, 2 * D), fine_attend, D)
     fine_gain_out[...] = gain_back(lay, lon, column, gain_f)
@@ -862,7 +868,7 @@
 def deep_scratch(lay, width):
     y, x, z = lay.y, lay.x, lay.z
     end = (lay.depth, width)
-    shapes = ((y, x, z), (z - 1, y, x), (y, x), (x - 1, y), (2, y, y), (2, y))
+    shapes = ((y, x, z), (z - 1, y, x), (y, x), (x - 1, y), (y, y), (2, y))
     return [pltpu.VMEM(shape + end, BF16) for shape in shapes]
 
 
@@ -889,8 +895,8 @@
         jnp.asarray(select, BF16),
         jnp.asarray(select.T, BF16),
     )
-    per_batch = 2 * (lay.x - 1 + lay.y - 1) + lay.z - 1 + 2 * lay.y - 1
-    deep_batch = lay.z - 1 + lay.x - 1 + 2 * lay.y - 1
+    per_batch = 2 * (lay.x - 1 + lay.y - 1) + lay.z - 1 + lay.y
+    deep_batch = lay.z - 1 + lay.x - 1 + lay.y
     copies = 5 * 8 + 7 + 2 * per_batch + deep_batch
     depth = lay.depth
     fine_shape = jax.ShapeDtypeStruct((2, lay.y, depth, lay.fine_width), BF16)

time: 79 us -> 78.6 us (level)
  no operation moved by 1% of the time
where the time goes in v7:
time: 78.6 us; the launch traced here: 78.5 us
  Pallas kernels  77.7 us (99%)
    pallas_call x1, Pallas kernels, per_device(): pl.pallas_call(functools.partial(kernel, lay), out_shape=(jax.ShapeDtypeS...  75.8 us
    pallas_call x1, Pallas kernels, per_device(): pl.pallas_call(functools.partial(finish, lay), out_shape=(jax.ShapeDtypeS...  1.9 us

profile of v7, /device:TPU:1, one launch (start us, length us, event | category | flops | bytes accessed | tf_op | source)
XLA Modules:
  0.0 78.5 jit_solution(5193839937677131920)
XLA Ops:
  0.6 75.8 %shard_map.214 = (bf16[1,6,6,512]{3,2,1,0:T(8,128)(2,1)}, bf16[1,12,12,512]{3,2,1,0:T(8,128)(2,1)}, f32[1,16]{1,0:T(1,128)}, f32[1,16]{1,0:T(1,128)}, bf16[2,4,1...) custom-call(bf16[1,12,12,512]{3,2,1,0:T(8,128)(2,1)} %tokens_hbm.1, ...), custom_call_target="tpu_custom_call" | custom-call | tf_op jit(solution)/shard_map/pallas_call | solution.py:903
  76.5 1.9 %shard_map.215 = (bf16[1,6,6,512]{3,2,1,0:T(8,128)(2,1)}, bf16[1,12,12,512]{3,2,1,0:T(8,128)(2,1)}, f32[1,16]{1,0:T(1,128)}, f32[16,1536]{1,0:T(8,128)}, f32[16,...) custom-call(bf16[1,6,6,512]{3,2,1,0:T(8,128)(2,1)} %get-tuple-element.25.refs_0, ...), custom_call_target="tpu_custom_call" | custom-call | tf_op jit(solution)/shard_map/pallas_call | solution.py:970
